TPU v7x, 32 devices: a whole 2x2x4 slice. The times are simulated.
32 devices in a mesh: groups: 2 (over x), dom: 16 (over z, y, core).
Axes of the slice: x: 2, y: 2, z: 4, core: 2. Of those that a mesh axis runs over, the one named last changes fastest.
Arguments:
- cells: bfloat16 [32768, 256], P(('groups', 'dom')), parts along dimension 0, may hold values from -6 to 6
- counts: int32 [32], P(('groups', 'dom')), parts along dimension 0, may hold values from 256 to 1024, as said below
- w_x: bfloat16 [256, 256], replicated, may hold values from -0.375 to 0.375
- w_fx: bfloat16 [256, 256], replicated, may hold values from -0.375 to 0.375
- w_slice: bfloat16 [32, 64], replicated, may hold values from -3.59375 to 3.59375
- w_temp: bfloat16 [32], replicated, may hold values from -1.1953125 to 1.1953125
- w_qkv: bfloat16 [3, 32, 32], replicated, may hold values from -1 to 1
- w_out: bfloat16 [256, 256], replicated, may hold values from -0.375 to 0.375
- cotangent: bfloat16 [32768, 256], P(('groups', 'dom')), parts along dimension 0, may hold values from -6 to 6
Outputs:
- result: bfloat16 [32768, 256], P(('groups', 'dom')), parts along dimension 0
- grad_cells: bfloat16 [32768, 256], P(('groups', 'dom')), parts along dimension 0
- grad_w_x: float32 [512, 256], P('groups'), parts along dimension 0
- grad_w_fx: float32 [512, 256], P('groups'), parts along dimension 0
- grad_w_slice: float32 [64, 64], P('groups'), parts along dimension 0
- grad_w_temp: float32 [64], P('groups'), parts along dimension 0
- grad_w_qkv: float32 [6, 32, 32], P('groups'), parts along dimension 0
- grad_w_out: float32 [512, 256], P('groups'), parts along dimension 0
There are 2 independent parts, one for each index of `groups`. A program takes and returns all parts, laid end to end along the dimension named above; an argument that names none is the same for every part. Nothing has to cross between parts.
Inputs may be any that keep to these rules, and one draw needn't show every extreme that they name: `counts`: entry p is the number of live cells of partition p; they are its first rows, the rest of its 1024 rows are padding; some partition is full.
All inputs are finite; a program needn't handle non-finite values.
Results may differ from a plain program's by a relative error of at most 0.012.
The roundings to bfloat16 on the way count: a program that leaves them out, or rounds other values in their place, can miss the bound.
Values may be sent and summed in bfloat16 or wider, within the bound.
A program may use at most 64 MiB of HBM per device.

v0:
```python
import math

import jax
import jax.numpy as jnp
from jax import lax
from jax.sharding import PartitionSpec as P

SLICES = 64


def matrix_product(form, left, right):
    return jnp.einsum(form, left, right, preferred_element_type=jnp.float32)


def slice_softmax(logits, temp_lin):
    temper = 0.5 + jax.nn.softplus(temp_lin)
    scaled = 10.0 * jnp.tanh(logits / 10.0) / temper
    powers = jnp.exp(scaled)
    return powers / jnp.sum(powers, axis=-1, keepdims=True)


def make_tokens(numerator_sums, denominators):
    return numerator_sums / (denominators[:, None] + 1e-05)


def project_tokens(tokens, qkv_weight):
    return jnp.einsum("rd,kde->kre", tokens, qkv_weight, precision=lax.Precision.HIGHEST)


def attend(query_rows, key_matrix, value_matrix):
    score_matrix = jnp.einsum(
        "zir,zjr->zij", query_rows, key_matrix, precision=lax.Precision.HIGHEST
    )
    score_matrix = score_matrix / math.sqrt(query_rows.shape[-1])
    powers = jnp.exp(10.0 * jnp.tanh(score_matrix / 10.0))
    attention_matrix = powers / jnp.sum(powers, axis=-1, keepdims=True)
    return jnp.einsum(
        "xwu,xut->xwt", attention_matrix, value_matrix, precision=lax.Precision.HIGHEST
    )


def mix_tokens(numerator_sums, denominators, qkv_weight):
    head_width = numerator_sums.shape[-1]
    maps = project_tokens(make_tokens(numerator_sums, denominators), qkv_weight)
    maps = maps.reshape(3, -1, SLICES, head_width)
    return attend(maps[0], maps[1], maps[2])


def cell_forward(cells, live_rows, w_x, w_fx, w_slice, w_temp):
    count_of_rows = cells.shape[0]
    head_width = w_slice.shape[0]
    count_of_heads = w_x.shape[1] // head_width
    projected = jnp.dot(cells, w_x, preferred_element_type=jnp.float32).astype(jnp.bfloat16)
    feature_rows = jnp.dot(cells, w_fx, preferred_element_type=jnp.float32).astype(jnp.bfloat16)
    per_head = projected.reshape(count_of_rows * count_of_heads, head_width)
    logits = jnp.dot(per_head, w_slice, preferred_element_type=jnp.float32)
    temp_lin = jnp.dot(per_head, w_temp.reshape(head_width, 1), preferred_element_type=jnp.float32)
    live_heads = jnp.repeat(live_rows, count_of_heads, axis=0)
    weight_matrix = (slice_softmax(logits, temp_lin) * live_heads).astype(jnp.bfloat16)
    weight_matrix = weight_matrix.reshape(count_of_rows, count_of_heads, -1)
    return (
        per_head,
        logits,
        temp_lin,
        live_heads,
        weight_matrix,
        feature_rows.reshape(count_of_rows, count_of_heads, head_width),
    )


def cell_backward(
    cells,
    per_head,
    logits,
    temp_lin,
    live_heads,
    weight_matrix,
    feature_rows,
    hidden_gradient3,
    mixed_lowp,
    numerator_gradient_lowp,
    denominator_gradient,
    w_x,
    w_fx,
    w_slice,
    w_temp,
):
    count_of_rows, count_of_heads, slice_count = weight_matrix.shape
    head_width = w_slice.shape[0]
    weight_gradient = matrix_product("fvo,vxo->fvx", hidden_gradient3, mixed_lowp)
    weight_gradient = (
        weight_gradient
        + matrix_product("fvo,vxo->fvx", feature_rows, numerator_gradient_lowp)
        + denominator_gradient[None]
    )
    feature_gradient = (
        matrix_product("rpc,pce->rpe", weight_matrix, numerator_gradient_lowp)
        .astype(jnp.bfloat16)
        .reshape(count_of_rows, -1)
    )
    _, soft_back = jax.vjp(slice_softmax, logits, temp_lin)
    d_logits, d_temp = soft_back(
        weight_gradient.reshape(count_of_rows * count_of_heads, slice_count) * live_heads
    )
    d_logits = d_logits.astype(jnp.bfloat16)
    d_temp = d_temp.astype(jnp.bfloat16)
    d_head = jnp.dot(d_logits, w_slice.T, preferred_element_type=jnp.float32)
    d_head = d_head + jnp.dot(
        d_temp, w_temp.reshape(1, head_width), preferred_element_type=jnp.float32
    )
    d_proj = d_head.reshape(count_of_rows, -1).astype(jnp.bfloat16)
    grad_cells = jnp.dot(d_proj, w_x.T, preferred_element_type=jnp.float32)
    grad_cells = (
        grad_cells + jnp.dot(feature_gradient, w_fx.T, preferred_element_type=jnp.float32)
    ).astype(jnp.bfloat16)
    grad_wx = jnp.dot(cells.T, d_proj, preferred_element_type=jnp.float32)
    grad_wfx = jnp.dot(cells.T, feature_gradient, preferred_element_type=jnp.float32)
    grad_slice = jnp.dot(per_head.T, d_logits, preferred_element_type=jnp.float32)
    grad_temp = jnp.dot(per_head.T, d_temp, preferred_element_type=jnp.float32).reshape(head_width)
    return (grad_cells, grad_wx, grad_wfx, grad_slice, grad_temp)


def body(cells, counts, w_x, w_fx, w_slice, w_temp, w_qkv, w_out, cotangent):
    count_of_rows, model_width = cells.shape
    positions = lax.iota(jnp.int32, count_of_rows)
    live_rows = (positions < counts[0]).astype(jnp.float32)[:, None]
    per_head, logits, temp_lin, live_heads, weight_matrix, feature_rows = cell_forward(
        cells, live_rows, w_x, w_fx, w_slice, w_temp
    )
    numerator_sums = matrix_product("skb,sko->kbo", weight_matrix, feature_rows)
    denominators = jnp.sum(weight_matrix, axis=0, dtype=jnp.float32)
    count_of_heads, slice_count, head_width = numerator_sums.shape
    flat_numer = numerator_sums.reshape(-1, head_width)
    flat_denom = denominators.reshape(-1)
    qkv_weight = w_qkv.astype(jnp.float32)
    total_numer, total_denom = lax.psum((flat_numer, flat_denom), "dom")
    mixed, mix_back = jax.vjp(mix_tokens, total_numer, total_denom, qkv_weight)
    mixed_lowp = mixed.astype(jnp.bfloat16)
    hidden_rows = (
        matrix_product("rpc,pce->rpe", weight_matrix, mixed_lowp)
        .astype(jnp.bfloat16)
        .reshape(count_of_rows, model_width)
    )
    result = jnp.dot(hidden_rows, w_out, preferred_element_type=jnp.float32).astype(jnp.bfloat16)
    hidden_gradient = jnp.dot(cotangent, w_out.T, preferred_element_type=jnp.float32).astype(
        jnp.bfloat16
    )
    hidden_gradient3 = hidden_gradient.reshape(count_of_rows, count_of_heads, head_width)
    out_grad = jnp.dot(hidden_rows.T, cotangent, preferred_element_type=jnp.float32)
    mixed_gradient = matrix_product("skb,sko->kbo", weight_matrix, hidden_gradient3)
    total_mixed = lax.psum(mixed_gradient, "dom")
    d_numer, denominator_gradient, d_qkv = mix_back(total_mixed)
    numerator_gradient_lowp = d_numer.reshape(count_of_heads, slice_count, head_width).astype(
        jnp.bfloat16
    )
    denominator_gradient = denominator_gradient.reshape(count_of_heads, slice_count)
    grad_cells, grad_wx, grad_wfx, grad_slice, grad_temp = cell_backward(
        cells,
        per_head,
        logits,
        temp_lin,
        live_heads,
        weight_matrix,
        feature_rows,
        hidden_gradient3,
        mixed_lowp,
        numerator_gradient_lowp,
        denominator_gradient,
        w_x,
        w_fx,
        w_slice,
        w_temp,
    )
    sum_wx, sum_wfx, sum_slice, sum_temp, total_out = lax.psum(
        (grad_wx, grad_wfx, grad_slice, grad_temp, out_grad), "dom"
    )
    scale = 1.0 / math.sqrt(count_of_rows * lax.axis_size("dom"))
    return (
        result,
        grad_cells,
        sum_wx * scale,
        sum_wfx * scale,
        sum_slice * scale,
        sum_temp * scale,
        d_qkv * scale,
        total_out * scale,
    )


def solution(mesh):
    placed = (
        P(("groups", "dom"), None),
        P(("groups", "dom")),
        P(),
        P(),
        P(),
        P(),
        P(),
        P(),
        P(("groups", "dom"), None),
    )
    return jax.shard_map(
        body,
        mesh=mesh,
        in_specs=placed,
        out_specs=(
            P(("groups", "dom"), None),
            P(("groups", "dom"), None),
            P("groups", None),
            P("groups", None),
            P("groups", None),
            P("groups"),
            P("groups", None, None),
            P("groups", None),
        ),
        check_vma=False,
    )
```

profile of v0, /device:TPU:0, one launch (start us, length us, event | category | flops | bytes accessed | tf_op | source)
XLA Modules:
  0.0 333.5 jit_solution(15764778787668835818)
XLA Ops:
  16.6 2.7 copy.40
  19.3 3.4 %copy.41 = bf16[1024,8,64]{0,2,1:T(8,128)(2,1)} copy(bf16[1024,8,64]{2,1,0:T(8,128)(2,1)} %bitcast.106) | data formatting | bytes 2097152 | tf_op jit(solution)/shard_map/reshape | solution.py:60
  23.9 1.6 fusion.36
  27.7 2.3 fusion.38
  30.1 2.7 convert_reduce_fusion
  33.5 35.2 %psum.57 = f32[512]{0:T(512)S(1)} all-reduce(f32[512]{0:T(512)S(1)} %reshape.140), channel_id=1, replica_groups=mesh['groups'=2,'dom'=16] {'dom'}, use_global_device_ids=true, to_apply=%region_3.4 | all-reduce | flops 512 | bytes 4096 | tf_op jit(solution)/shard_map/psum | solution.py:136
  69.3 53.4 %all-reduce.11.cloned.1.call-done = (f32[512,32]{0,1:T(8,128)}, f32[8,64,32]{1,2,0:T(8,128)}) async-done(((f32[512,32]{0,1:T(8,128)}, f32[8,64,32]{1,2,0:T(8,128)}), (f32[512,32]{0,1:T(8,128)}, f32[8,64,32]{1,2,0:T(8,128)})) %all-reduce.11.cloned.1.call-update) | async-done | bytes 131088 | tf_op jit(solution)/shard_map/psum | solution.py:136
  125.9 1.6 fusion.6
  127.6 1.6 squeeze.15
  129.1 1.5 convolution_bitcast_fusion.4
  130.7 1.6 multiply_reduce_fusion.2
  132.3 1.5 convolution_bitcast_fusion.3
  134.8 1.8 fusion.37
  138.9 1.5 convolution_convert_fusion
  140.4 3.6 %add_bitcast_fusion = f32[1024,8,64]{0,2,1:T(8,128)} fusion(f32[8,64,1024]{2,1,0:T(8,128)} %fusion.37, bf16[1024,8,32]{0,2,1:T(8,128)(2,1)} %bitcast.115, f32[8,64]{1,0:T(8,128)S(1)} %neg.38, bf16[8,64,32]{1,0,2:T(8,128)(2,1)S(1)} %convert_element_type.70), kind=kOutput, calls=%fused_computation.9 | convolution fusion | flops 34603008 | bytes 4753408 | tf_op jit(solution)/shard_map/fvo,vxo->fvx/dot_general | solution.py:12
  144.0 3.8 %copy.58 = f32[1024,8,64]{2,1,0:T(8,128)} copy(f32[1024,8,64]{0,2,1:T(8,128)} %add_bitcast_fusion) | data formatting | bytes 4194304 | tf_op jit(solution)/shard_map/add | solution.py:92
  147.8 3.8 %copy.59 = f32[8192,64]{0,1:T(8,128)} copy(f32[8192,64]{1,0:T(8,128)} %bitcast.107) | data formatting | bytes 4194304 | tf_op jit(solution)/shard_map/reshape | solution.py:103
  151.7 3.0 multiply_reduce_fusion.1
  158.4 2.6 copy.60
  161.0 3.9 %convert_element_type.74 = bf16[1024,256]{1,0:T(8,128)(2,1)} reshape(bf16[8192,32]{1,0:T(8,128)(2,1)} %copy.60) | data formatting | bytes 1048576 | tf_op jit(solution)/shard_map/convert_element_type | solution.py:111
  164.9 2.2 convolution_bitcast_fusion.1
  167.1 2.4 fusion.39
  172.8 58.7 %all-reduce.3 = (f32[32,64]{1,0:T(8,128)S(1)}, f32[32]{0:T(128)S(1)}) all-reduce(f32[32,64]{1,0:T(8,128)S(1)} %fusion.40, f32[32]{0:T(128)S(1)} %convolution_bitcast_fusion.6), channel_id=1, replica_groups=mesh['groups'=2,'dom'=16] {'dom'}, use_global_device_ids=true, to_apply=%region_12.13 | all-reduce | flops 2080 | bytes 16640 | tf_op jit(solution)/shard_map/psum | solution.py:174
  234.7 88.3 %all-reduce.9.cloned.1.call-done = (f32[256,256]{0,1:T(8,128)}, f32[256,256]{0,1:T(8,128)}, f32[256,256]{0,1:T(8,128)}) async-done(((f32[256,256]{0,1:T(8,128)}, f32[256,256]{0,1:T(8,128)}, f32[256,256]{0,1:T(8,128)}), (f32[256,256]{0,1:T(8,128)}, f32[256,256]{0,1:T(8,128)}, f32[256,256]{0,1:T(8,128)})) %all-reduce.9.cloned.1.call-update) | async-done | bytes 786448 | tf_op jit(solution)/shard_map/psum | solution.py:174
  (110 shorter events, 33.6 us)
Async XLA Ops:
  7.2 3.1 copy-start.24
  7.2 115.5 %all-reduce.11.cloned.1.call-start = ((), (), s32[]{:S(2)}) async-start(), calls=%async_computation.1 | async-start | bytes 393216 | tf_op jit(solution)/shard_map/psum | solution.py:136
  10.3 2.4 copy-start.22
  13.8 1.3 copy-start.3
  19.3 3.4 %copy-start.12 = (bf16[256,256]{1,0:T(8,128)(2,1)S(1)}, bf16[256,256]{1,0:T(8,128)(2,1)}, u32[]{:S(2)}) copy-start(bf16[256,256]{1,0:T(8,128)(2,1)} %param.12) | copy-start | bytes 393220
  22.7 3.6 %copy-start.10 = (bf16[256,256]{1,0:T(8,128)(2,1)S(1)}, bf16[256,256]{1,0:T(8,128)(2,1)}, u32[]{:S(2)}) copy-start(bf16[256,256]{1,0:T(8,128)(2,1)} %param.16) | copy-start | bytes 393220
  27.7 41.5 %copy-start.20 = (bf16[3,32,32]{2,1,0:T(8,128)(2,1)S(1)}, bf16[3,32,32]{2,1,0:T(8,128)(2,1)}, u32[]{:S(2)}) copy-start(bf16[3,32,32]{2,1,0:T(8,128)(2,1)} %param.15) | copy-start | bytes 18436
  30.0 293.0 %all-reduce.9.cloned.1.call-start = ((), (), s32[]{:S(2)}) async-start(), calls=%async_computation | async-start | bytes 1572864 | tf_op jit(solution)/shard_map/psum | solution.py:174
  129.1 4.7 %copy-start.15 = (f32[8,64,32]{1,0,2:T(8,128)S(1)}, f32[8,64,32]{1,0,2:T(8,128)}, u32[]{:S(2)}) copy-start(f32[8,64,32]{1,0,2:T(8,128)} %squeeze.14) | copy-start | bytes 196612
  130.6 3.7 %copy-start.14 = (f32[8,64,32]{1,0,2:T(8,128)S(1)}, f32[8,64,32]{1,0,2:T(8,128)}, u32[]{:S(2)}) copy-start(f32[8,64,32]{1,0,2:T(8,128)} %squeeze.15) | copy-start | bytes 196612
  134.3 2.2 copy-start.1
  136.6 1.5 copy-start.9
  136.6 1.8 copy-start.21
  147.8 3.8 %copy-start.19 = (f32[8192]{0:T(1024)S(1)}, f32[8192]{0:T(1024)}, u32[]{:S(2)}) copy-start(f32[8192]{0:T(1024)} %multiply_divide_fusion.1) | copy-start | bytes 98308
  151.6 3.0 copy-start.2
  151.6 3.5 %copy-start.4 = (f32[8192,64]{0,1:T(8,128)S(1)}, f32[8192,64]{0,1:T(8,128)}, u32[]{:S(2)}) copy-start(f32[8192,64]{0,1:T(8,128)} %copy-done.3) | copy-start | bytes 6291460
  151.6 3.5 %copy-start.18 = (f32[8192]{0:T(1024)S(1)}, f32[8192]{0:T(1024)}, u32[]{:S(2)}) copy-start(f32[8192]{0:T(1024)} %get-tuple-element.40) | copy-start | bytes 98308
  161.0 6.1 %copy-start.16 = (bf16[256,256]{1,0:T(8,128)(2,1)S(1)}, bf16[256,256]{1,0:T(8,128)(2,1)}, u32[]{:S(2)}) copy-start(bf16[256,256]{1,0:T(8,128)(2,1)} %param.11) | copy-start | bytes 393220
  164.9 4.5 %copy-start.5 = (bf16[8,32,1024]{2,1,0:T(8,128)(2,1)S(1)}, bf16[8,32,1024]{2,1,0:T(8,128)(2,1)}, u32[]{:S(2)}) copy-start(bf16[8,32,1024]{2,1,0:T(8,128)(2,1)} %convolution_convert_fusion.3) | copy-start | bytes 1572868
  164.9 4.5 %copy-start.8 = (bf16[1024,256]{1,0:T(8,128)(2,1)S(1)}, bf16[1024,256]{1,0:T(8,128)(2,1)}, u32[]{:S(2)}) copy-start(bf16[1024,256]{1,0:T(8,128)(2,1)} %param.17) | copy-start | bytes 1572868
  164.9 5.6 %copy-start.11 = (bf16[256,256]{1,0:T(8,128)(2,1)S(1)}, bf16[256,256]{1,0:T(8,128)(2,1)}, u32[]{:S(2)}) copy-start(bf16[256,256]{1,0:T(8,128)(2,1)} %param.16) | copy-start | bytes 393220
  172.4 61.2 %copy-start.13 = (bf16[256,256]{1,0:T(8,128)(2,1)S(1)}, bf16[256,256]{1,0:T(8,128)(2,1)}, u32[]{:S(2)}) copy-start(bf16[256,256]{1,0:T(8,128)(2,1)} %param.12) | copy-start | bytes 393220
  172.8 60.8 %copy-start.7 = (f32[1024,256]{1,0:T(8,128)S(1)}, f32[1024,256]{1,0:T(8,128)}, u32[]{:S(2)}) copy-start(f32[1024,256]{1,0:T(8,128)} %fusion.39) | copy-start | bytes 3145732
  323.0 2.8 copy-start.17
  (4 other events, 3.4 us)
Sparse Core Ops, SparseCore 0:
  30.2 92.5 all-reduce.10
  233.2 89.7 all-reduce.8
where the time goes:
time: 334 us; the launch traced here: 333 us
  waiting for transfers between devices  142 us (43%)
  blocking collectives  93.8 us (28%)
  matrix products  36.2 us (11%)
  local copies, waits for them, and re-layouts  33.8 us (10%)
  between operations  15.1 us (5%)
  other arithmetic  12.6 us (4%)
    psum x1, waiting for transfers between devices, body(): lax.psum((grad_wx, grad_wfx, grad_slice, grad_temp, out_grad), 'dom')  88.3 us
    psum x1, blocking collectives, body(): lax.psum((grad_wx, grad_wfx, grad_slice, grad_temp, out_grad), 'dom')  58.7 us
    psum x1, waiting for transfers between devices, body(): total_numer, total_denom = lax.psum((flat_numer, flat_denom), 'dom')  53.4 us
    psum x1, blocking collectives, body(): total_numer, total_denom = lax.psum((flat_numer, flat_denom), 'dom')  35.2 us
    dot_general x6, matrix products, matrix_product(): return jnp.einsum(form, left, right, preferred_element_type=jnp.float32)  11.9 us
    unnamed x57, local copies, waits for them, and re-layouts  6.96 us
  transfers between devices with their start and end apart: 2, of which 2 were waited for; matrix products, arithmetic and copies ran while one was open for 2% of the time, Pallas kernels for 0%

commit v1 on v0

v1 whole, which is shorter than its diff:
```python
import functools
import math

import jax
import jax.numpy as jnp
from jax import lax
from jax.experimental import pallas as pl
from jax.experimental.pallas import tpu as pltpu
from jax.sharding import PartitionSpec as P

HEAD = 32
SLICES = 64
HEADS = 8
WIDTH = HEAD * HEADS
SPREAD = SLICES * HEADS
HALF = WIDTH // 2
CHUNK = 256
F32 = jnp.float32
BF16 = jnp.bfloat16
MESH = pl.DeviceIdType.MESH


def mm(left, right):
    return jnp.dot(left, right, preferred_element_type=F32)


def mm_nt(left, right):
    return lax.dot_general(left, right, (((1,), (1,)), ((), ())), preferred_element_type=F32)


def mm_tn(left, right):
    return lax.dot_general(left, right, (((0,), (0,)), ((), ())), preferred_element_type=F32)


def split(value):
    high = value.astype(BF16)
    return high, (value - high.astype(F32)).astype(BF16)


def pick2(value, ones):
    high, low = split(value)
    return mm(high, ones) + mm(low, ones)


def pick3(value, ones, product=mm):
    high = value.astype(BF16)
    rest = value - high.astype(F32)
    middle, low = split(rest)
    return product(high, ones) + product(middle, ones) + product(low, ones)


def wide(left, right, product):
    left_high, left_low = split(left)
    right_high, right_low = split(right)
    return (
        product(left_high, right_high)
        + product(left_high, right_low)
        + product(left_low, right_high)
    )


def block_mask(shape, row_width, column_width):
    rows = lax.broadcasted_iota(jnp.int32, shape, 0)
    columns = lax.broadcasted_iota(jnp.int32, shape, 1)
    return (rows // row_width) == (columns // column_width)


def stages_of(devices, rows, tile):
    sizes, rest = [2], devices // 2
    while rest > 1:
        size = min(8, rest)
        sizes.append(size)
        rest //= size
    stages, stride = [], 1
    for size in sizes:
        scattered = rows % (size * tile) == 0
        stages.append((size, stride, rows, scattered))
        rows = rows // size if scattered else rows
        stride *= size
    return stages


def peers_of(stage):
    size, stride, _, _ = stage
    me = lax.axis_index("dom")
    place = lax.rem(lax.div(me, stride), size)
    others = []
    for step in range(1, size):
        there = lax.rem(place + step, size)
        others.append((there, me + (there - place) * stride))
    return place, others


class Reduction:
    @staticmethod
    def scratch(stages, columns, dtype):
        shapes = []
        for size, _, rows, scattered in stages:
            part = rows // size if scattered else rows
            shapes += [
                pltpu.VMEM((rows, columns), dtype),
                pltpu.VMEM((size, part, columns), dtype),
                pltpu.VMEM((rows, columns), dtype),
                pltpu.SemaphoreType.DMA((4, size)),
            ]
        return shapes

    def __init__(self, stages, refs):
        self.stages = stages
        self.levels = [refs[4 * i : 4 * i + 4] for i in range(len(stages))]

    def source(self):
        return self.levels[0][0]

    def total(self):
        return self.levels[0][2]

    def send(self, index):
        stage = self.stages[index]
        size, _, rows, scattered = stage
        source, received, _, sems = self.levels[index]
        place, others = peers_of(stage)
        part = rows // size if scattered else rows
        self.flying = []
        for step, (there, device) in enumerate(others):
            cut = source
            if scattered:
                cut = source.at[pl.ds(pl.multiple_of(there * part, part), part), :]
            copy = pltpu.make_async_remote_copy(
                src_ref=cut,
                dst_ref=received.at[place],
                send_sem=sems.at[0, step],
                recv_sem=sems.at[1, step],
                device_id={"dom": device},
                device_id_type=MESH,
            )
            copy.start()
            self.flying.append(copy)
        if scattered:
            received[place] = source[pl.ds(pl.multiple_of(place * part, part), part), :]
        else:
            received[place] = source[...]

    def fold(self, index):
        size, _, rows, scattered = self.stages[index]
        source, received, gathered, _ = self.levels[index]
        for copy in self.flying:
            copy.wait()
        total = received[0].astype(F32)
        for slot in range(1, size):
            total = total + received[slot].astype(F32)
        total = total.astype(source.dtype)
        if index + 1 < len(self.stages):
            self.levels[index + 1][0][...] = total
        else:
            self.place(index, total)

    def place(self, index, value):
        size, _, rows, scattered = self.stages[index]
        gathered = self.levels[index][2]
        if scattered:
            part = rows // size
            place, _ = peers_of(self.stages[index])
            gathered[pl.ds(pl.multiple_of(place * part, part), part), :] = value
        else:
            gathered[...] = value

    def gather(self, index):
        stage = self.stages[index]
        size, _, rows, scattered = stage
        gathered, sems = self.levels[index][2:]
        self.flying = []
        if not scattered:
            return
        part = rows // size
        place, others = peers_of(stage)
        mine = gathered.at[pl.ds(pl.multiple_of(place * part, part), part), :]
        for step, (_, device) in enumerate(others):
            copy = pltpu.make_async_remote_copy(
                src_ref=mine,
                dst_ref=mine,
                send_sem=sems.at[2, step],
                recv_sem=sems.at[3, step],
                device_id={"dom": device},
                device_id_type=MESH,
            )
            copy.start()
            self.flying.append(copy)

    def settle(self, index):
        for copy in self.flying:
            copy.wait()
        if index > 0:
            self.place(index - 1, self.levels[index][2][...])

    def last(self):
        return len(self.stages) - 1


def layer_kernel(
    token_stages,
    grad_stages,
    scale,
    counts_ref,
    cells_ref,
    cot_ref,
    wx_ref,
    wfx_ref,
    wslice_ref,
    wtemp_ref,
    wqkv_ref,
    wout_ref,
    result_ref,
    gcells_ref,
    gwx_ref,
    gwfx_ref,
    gslice_ref,
    gtemp_ref,
    gqkv_ref,
    gout_ref,
    proj_ref,
    feat_ref,
    dhid_ref,
    weight_ref,
    prob_ref,
    tanh_ref,
    scaled_ref,
    inverse_ref,
    sigmoid_ref,
    slice_bd,
    temp_bd,
    temp_row,
    acc_tokens,
    acc_out,
    acc_cells,
    acc_slice,
    acc_temp,
    mixed_bd,
    dnumer_bd,
    *sum_refs,
):
    rows = cells_ref.shape[0]
    chunks = rows // CHUNK
    levels = 4 * len(token_stages)
    levels_g = 4 * len(grad_stages)
    token_sum = Reduction(token_stages, sum_refs[:levels])
    early_sum = Reduction(grad_stages, sum_refs[levels : levels + levels_g])
    late_sum = Reduction(grad_stages, sum_refs[levels + levels_g :])

    barrier = pltpu.get_barrier_semaphore()
    greeted = 0
    for stage in token_stages:
        for _, device in peers_of(stage)[1]:
            pl.semaphore_signal(barrier, inc=1, device_id={"dom": device}, device_id_type=MESH)
            greeted += 1

    count = counts_ref[0]
    repeat32 = (
        (lax.broadcasted_iota(jnp.int32, (HEAD, WIDTH), 1) % HEAD)
        == lax.broadcasted_iota(jnp.int32, (HEAD, WIDTH), 0)
    ).astype(BF16)
    repeat64 = (
        (lax.broadcasted_iota(jnp.int32, (SLICES, SPREAD), 1) % SLICES)
        == lax.broadcasted_iota(jnp.int32, (SLICES, SPREAD), 0)
    ).astype(BF16)
    diag_slice = block_mask((WIDTH, SPREAD), HEAD, SLICES)
    tall = mm_tn(repeat32, wslice_ref[...]).astype(BF16)
    slice_bd[...] = jnp.where(diag_slice, mm(tall, repeat64), 0.0).astype(BF16)
    temp_rows = jnp.broadcast_to(wtemp_ref[...], (128, HEAD))
    temp_bd[...] = jnp.where(
        block_mask((WIDTH, 128), HEAD, 1), mm_nt(repeat32.T, temp_rows), 0.0
    ).astype(BF16)
    temp_row[...] = jnp.where(
        block_mask((128, WIDTH), 1, HEAD), mm(temp_rows, repeat32), 0.0
    ).astype(BF16)
    gather_heads = block_mask((SPREAD, 128), SLICES, 1).astype(BF16)
    spread_heads = block_mask((128, SPREAD), 1, SLICES).astype(BF16)
    half_diag = block_mask((256, HALF), SLICES, HEAD)

    acc_tokens[...] = jnp.zeros_like(acc_tokens)
    acc_out[...] = jnp.zeros_like(acc_out)
    acc_cells[...] = jnp.zeros_like(acc_cells)
    acc_slice[...] = jnp.zeros_like(acc_slice)
    acc_temp[...] = jnp.zeros_like(acc_temp)

    def cut(index):
        return pl.ds(pl.multiple_of(index * CHUNK, CHUNK), CHUNK)

    def live_of(index):
        place = lax.broadcasted_iota(jnp.int32, (CHUNK, 1), 0) + index * CHUNK
        return (place < count).astype(F32)

    def forward(index, carry):
        part = cut(index)
        cells = cells_ref[part, :]
        projected = mm(cells, wx_ref[...]).astype(BF16)
        features = mm(cells, wfx_ref[...]).astype(BF16)
        d_hidden = mm_nt(cot_ref[part, :], wout_ref[...]).astype(BF16)
        logits = mm(projected, slice_bd[...])
        temp_lin = mm(projected, temp_bd[...])
        away = jnp.exp(-jnp.abs(temp_lin))
        temper = 0.5 + (jnp.maximum(temp_lin, 0.0) + jnp.log(1.0 + away))
        inverse = 1.0 / temper
        sigmoid = jnp.where(temp_lin >= 0.0, 1.0, away) / (1.0 + away)
        bent = jnp.tanh(logits / 10.0)
        scaled = (10.0 * bent) * pick2(inverse, spread_heads)
        powers = jnp.exp(scaled)
        sums = pick2(powers, gather_heads)
        used = lax.broadcasted_iota(jnp.int32, (CHUNK, 128), 1) < HEADS
        over = live_of(index) / jnp.where(used, sums, 1.0)
        probs = powers * pick2(over, spread_heads)
        weights = probs.astype(BF16)
        proj_ref[part, :] = projected
        feat_ref[part, :] = features
        dhid_ref[part, :] = d_hidden
        weight_ref[part, :] = weights
        prob_ref[part, :] = probs
        tanh_ref[part, :] = bent
        scaled_ref[part, :] = scaled
        inverse_ref[part, :] = inverse
        sigmoid_ref[part, :] = sigmoid
        ones = jnp.ones((CHUNK, 128), BF16)
        for half in range(2):
            lanes = slice(half * HALF, (half + 1) * HALF)
            right = jnp.concatenate([features[:, lanes], d_hidden[:, lanes], ones], axis=1)
            acc_tokens[half] += mm_tn(weights[:, half * 256 : (half + 1) * 256], right)
        return carry

    lax.fori_loop(0, chunks, forward, 0)

    payload = token_sum.source()
    lane = lax.broadcasted_iota(jnp.int32, (SLICES, 128), 1)
    totals = jnp.zeros((SLICES, 128), F32)
    for half in range(2):
        lanes = slice(half * HALF, (half + 1) * HALF)
        numer = jnp.where(half_diag, acc_tokens[half, :, 0:HALF], 0.0)
        dmix = jnp.where(half_diag, acc_tokens[half, :, HALF : 2 * HALF], 0.0)
        payload[0:SLICES, lanes] = sum(numer[i * 64 : i * 64 + 64] for i in range(4))
        payload[SLICES : 2 * SLICES, lanes] = sum(dmix[i * 64 : i * 64 + 64] for i in range(4))
        for i in range(4):
            block = acc_tokens[half, i * 64 : i * 64 + 64, 2 * HALF : 2 * HALF + 128]
            totals = totals + jnp.where(lane == half * 4 + i, block, 0.0)
    payload[0:SLICES, WIDTH : WIDTH + 128] = totals
    payload[SLICES : 2 * SLICES, WIDTH : WIDTH + 128] = jnp.zeros((SLICES, 128), F32)

    pl.semaphore_wait(barrier, greeted)
    for index in range(len(token_stages)):
        token_sum.send(index)
        token_sum.fold(index)
    for index in reversed(range(len(token_stages))):
        token_sum.gather(index)
        token_sum.settle(index)

    total = token_sum.total()
    numerators = total[0:SLICES, 0:WIDTH]
    d_mixed = total[SLICES : 2 * SLICES, 0:WIDTH]
    spread32 = block_mask((128, WIDTH), 1, HEAD).astype(BF16)
    denominators = pick3(total[0:SLICES, WIDTH : WIDTH + 128], spread32) + 1e-05
    tokens = numerators / denominators
    diag_square = block_mask((WIDTH, WIDTH), HEAD, HEAD)
    diag_tall = block_mask((SPREAD, WIDTH), SLICES, HEAD)
    maps = []
    for k in range(3):
        stacked = mm_tn(repeat32, wqkv_ref[k]).astype(BF16)
        maps.append(jnp.where(diag_square, mm(stacked, repeat32), 0.0).astype(BF16))


    queries, key_rows, value_rows = [
        pick3(tokens, weight) for weight in maps
    ]

    def expand(value):
        return jnp.where(diag_tall, jnp.concatenate([value] * HEADS, axis=0), 0.0)

    def contract(value):
        value = jnp.where(diag_tall, value, 0.0)
        return sum(value[i * SLICES : (i + 1) * SLICES] for i in range(HEADS))

    keys_bd = expand(key_rows)
    values_bd = expand(value_rows)
    root = 1.0 / math.sqrt(HEAD)
    bent = jnp.tanh(wide(queries, keys_bd, mm_nt) * root / 10.0)
    powers = jnp.exp(10.0 * bent)
    sums = pick3(powers, gather_heads)
    used = lax.broadcasted_iota(jnp.int32, (SLICES, 128), 1) < HEADS
    attention = powers * pick3(1.0 / jnp.where(used, sums, 1.0), spread_heads)
    mixed_low = wide(attention, values_bd, mm).astype(BF16)
    mixed_bd[...] = expand(mixed_low.astype(F32)).astype(BF16)

    d_attention = wide(d_mixed, values_bd, mm_nt)
    d_values = contract(wide(attention, d_mixed, mm_tn))
    shared = attention * d_attention
    shared = shared - attention * pick3(pick3(shared, gather_heads), spread_heads)
    d_scores = shared * (1.0 - bent * bent) * root
    d_queries = wide(d_scores, keys_bd, mm)
    d_keys = contract(wide(d_scores, queries, mm_tn))
    d_maps = (d_queries, d_keys, d_values)
    d_tokens = sum(pick3(d, weight, mm_nt) for d, weight in zip(d_maps, maps))
    d_numer = d_tokens / denominators
    dnumer_bd[...] = expand(d_numer).astype(BF16)
    d_denom = pick3(
        -expand(d_numer * tokens), jnp.ones((128, WIDTH), BF16),
        lambda value, ones: mm_nt(ones, value),
    )[0:1, :]
    for k in range(3):
        square = jnp.where(diag_square, wide(tokens, d_maps[k], mm_tn), 0.0)
        strip = sum(square[i * HEAD : (i + 1) * HEAD] for i in range(HEADS))
        gqkv_ref[k] = pick3(strip, repeat32, mm_nt) * scale

    def early(index, carry):
        part = cut(index)
        weights = weight_ref[part, :]
        cot = cot_ref[part, :]
        hidden = mm(weights, mixed_bd[...]).astype(BF16)
        d_features = mm(weights, dnumer_bd[...]).astype(BF16)
        result_ref[part, :] = mm(hidden, wout_ref[...]).astype(BF16)
        dfeat = mm_nt(d_features, wfx_ref[...])
        acc_out[:, 0:WIDTH] += mm_tn(hidden, cot)
        acc_out[:, WIDTH : 2 * WIDTH] += mm_tn(cells_ref[part, :], d_features)
        scaled = scaled_ref[part, :]
        probs = prob_ref[part, :]
        bent = tanh_ref[part, :]
        inverse = inverse_ref[part, :]
        d_weights = (
            mm_nt(dhid_ref[part, :], mixed_bd[...])
            + mm_nt(feat_ref[part, :], dnumer_bd[...])
            + d_denom
        )
        shared = probs * d_weights
        shared = shared - probs * pick2(pick2(shared, gather_heads), spread_heads)
        d_logits = (
            shared * (1.0 - bent * bent) * pick2(inverse, spread_heads)
        ).astype(BF16)
        d_temper = -pick2(shared * scaled, gather_heads) * inverse
        d_temp = (d_temper * sigmoid_ref[part, :]).astype(BF16)
        d_proj = (mm_nt(d_logits, slice_bd[...]) + mm(d_temp, temp_row[...])).astype(BF16)
        gcells_ref[part, :] = (mm_nt(d_proj, wx_ref[...]) + dfeat).astype(BF16)
        acc_cells[...] += mm_tn(cells_ref[part, :], d_proj)
        projected = proj_ref[part, :]
        acc_temp[...] += mm_tn(projected, d_temp)
        for half in range(2):
            acc_slice[half] += mm_tn(
                projected[:, half * HALF : (half + 1) * HALF],
                d_logits[:, half * 256 : (half + 1) * 256],
            )
        return carry

    lax.fori_loop(0, chunks, early, 0)

    early_sum.source()[...] = acc_out[...].astype(BF16)
    early_sum.send(0)
    late = late_sum.source()
    late[:, 0:WIDTH] = acc_cells[...].astype(BF16)
    own = jnp.where(block_mask((WIDTH, 128), HEAD, 1), acc_temp[...], 0.0)
    own = jnp.sum(own, axis=1, keepdims=True)
    for half in range(2):
        block = jnp.where(block_mask((HALF, 256), HEAD, SLICES), acc_slice[half], 0.0)
        block = block[:, 0:128] + block[:, 128:256]
        block = block + pltpu.roll(block, 64, 1)
        lanes = lax.broadcasted_iota(jnp.int32, (HALF, 128), 1)
        here = slice(half * HALF, (half + 1) * HALF)
        late[here, WIDTH : WIDTH + 128] = jnp.where(lanes < SLICES, block, own[here]).astype(BF16)
    late_sum.send(0)

    for index in range(len(grad_stages)):
        early_sum.fold(index)
        if index < early_sum.last():
            early_sum.send(index + 1)
        else:
            early_sum.gather(index)
        late_sum.fold(index)
        if index < late_sum.last():
            late_sum.send(index + 1)
        else:
            late_sum.gather(index)
    for index in reversed(range(len(grad_stages))):
        early_sum.settle(index)
        if index > 0:
            early_sum.gather(index - 1)
        else:
            gout_ref[...] = early_sum.total()[:, 0:WIDTH].astype(F32) * scale
            gwfx_ref[...] = early_sum.total()[:, WIDTH : 2 * WIDTH].astype(F32) * scale
        late_sum.settle(index)
        if index > 0:
            late_sum.gather(index - 1)
    gwx_ref[...] = late_sum.total()[:, 0:WIDTH].astype(F32) * scale
    extra = late_sum.total()[:, WIDTH : WIDTH + 128].astype(F32)
    extra = sum(extra[i * HEAD : (i + 1) * HEAD] for i in range(HEADS)) * scale
    gslice_ref[...] = extra[:, 0:SLICES]
    unit = (
        lax.broadcasted_iota(jnp.int32, (HEAD, HEAD), 0)
        == lax.broadcasted_iota(jnp.int32, (HEAD, HEAD), 1)
    ).astype(BF16)
    gtemp_ref[...] = pick3(extra, unit, mm_tn)[SLICES : SLICES + 1, :]


def body(devices, cells, counts, w_x, w_fx, w_slice, w_temp, w_qkv, w_out, cotangent):
    rows = cells.shape[0]
    token_stages = stages_of(devices, 2 * SLICES, 8)
    grad_stages = stages_of(devices, WIDTH, 16)
    scale = 1.0 / math.sqrt(rows * devices)
    vmem = pl.BlockSpec(memory_space=pltpu.VMEM)
    shape = jax.ShapeDtypeStruct
    outs = pl.pallas_call(
        functools.partial(layer_kernel, token_stages, grad_stages, scale),
        out_shape=(
            shape((rows, WIDTH), BF16),
            shape((rows, WIDTH), BF16),
            shape((WIDTH, WIDTH), F32),
            shape((WIDTH, WIDTH), F32),
            shape((HEAD, SLICES), F32),
            shape((1, HEAD), F32),
            shape((3, HEAD, HEAD), F32),
            shape((WIDTH, WIDTH), F32),
        ),
        in_specs=[pl.BlockSpec(memory_space=pltpu.SMEM)] + [vmem] * 8,
        out_specs=[vmem] * 8,
        scratch_shapes=[
            pltpu.VMEM((rows, WIDTH), BF16),
            pltpu.VMEM((rows, WIDTH), BF16),
            pltpu.VMEM((rows, WIDTH), BF16),
            pltpu.VMEM((rows, SPREAD), BF16),
            pltpu.VMEM((rows, SPREAD), F32),
            pltpu.VMEM((rows, SPREAD), F32),
            pltpu.VMEM((rows, SPREAD), F32),
            pltpu.VMEM((rows, 128), F32),
            pltpu.VMEM((rows, 128), F32),
            pltpu.VMEM((WIDTH, SPREAD), BF16),
            pltpu.VMEM((WIDTH, 128), BF16),
            pltpu.VMEM((128, WIDTH), BF16),
            pltpu.VMEM((2, 256, 2 * HALF + 128), F32),
            pltpu.VMEM((WIDTH, 2 * WIDTH), F32),
            pltpu.VMEM((WIDTH, WIDTH), F32),
            pltpu.VMEM((2, HALF, 256), F32),
            pltpu.VMEM((WIDTH, 128), F32),
            pltpu.VMEM((SPREAD, WIDTH), BF16),
            pltpu.VMEM((SPREAD, WIDTH), BF16),
        ]
        + Reduction.scratch(token_stages, WIDTH + 128, F32)
        + Reduction.scratch(grad_stages, 2 * WIDTH, BF16)
        + Reduction.scratch(grad_stages, WIDTH + 128, BF16),
        compiler_params=pltpu.CompilerParams(
            collective_id=0, has_side_effects=True, vmem_limit_bytes=44 * 1024 * 1024
        ),
    )(counts, cells, cotangent, w_x, w_fx, w_slice, w_temp.reshape(1, HEAD), w_qkv, w_out)
    result, gcells, gwx, gwfx, gslice, gtemp, gqkv, gout = outs
    return result, gcells, gwx, gwfx, gslice, gtemp.reshape(HEAD), gqkv, gout


def solution(mesh):
    placed = (
        P(("groups", "dom"), None),
        P(("groups", "dom")),
        P(),
        P(),
        P(),
        P(),
        P(),
        P(),
        P(("groups", "dom"), None),
    )
    return jax.shard_map(
        functools.partial(body, mesh.shape["dom"]),
        mesh=mesh,
        in_specs=placed,
        out_specs=(
            P(("groups", "dom"), None),
            P(("groups", "dom"), None),
            P("groups", None),
            P("groups", None),
            P("groups", None),
            P("groups"),
            P("groups", None, None),
            P("groups", None),
        ),
        check_vma=False,
    )
```

time: 334 us -> 63.5 us (0.19)
  waiting for transfers between devices: 142 us -> 0 us
  blocking collectives: 93.8 us -> 0 us
  Pallas kernels: 0 us -> 49.5 us
  matrix products: 36.2 us -> 0 us
  local copies, waits for them, and re-layouts: 33.8 us -> 12.3 us
  between operations: 15.1 us -> 1.31 us
  other arithmetic: 12.6 us -> 0 us
    psum x2 -> x0, waiting for transfers between devices: 142 us -> none  [the longest x1 88.3 us: body(): lax.psum((grad_wx, grad_wfx, grad_slice, grad_temp, out_grad), 'dom')]
    psum x2 -> x0, blocking collectives: 93.8 us -> none  [the longest x1 58.7 us: body(): lax.psum((grad_wx, grad_wfx, grad_slice, grad_temp, out_grad), 'dom')]
    pallas_call x0 -> x1, Pallas kernels: none -> 49.5 us  [body(): pl.pallas_call(functools.partial(layer_kernel, token_stages, grad_stages,...]
    dot_general x28 -> x0, matrix products: 35.2 us -> none  [the longest x6 11.9 us: matrix_product(): return jnp.einsum(form, left, right, preferred_element_type=jnp.float32)]
    convert_element_type x5 -> x0, local copies, waits for them, and re-layouts: 9.38 us -> none  [the longest x2 6.51 us: cell_backward(): d_proj = d_head.reshape(count_of_rows, -1).astype(jnp.bfloat16)]
    reshape x6 -> x0, local copies, waits for them, and re-layouts: 9.08 us -> none  [the longest x1 3.83 us: cell_backward(): weight_gradient.reshape(count_of_rows * count_of_heads, slice_count)]
    reduce_sum x3 -> x0, other arithmetic: 7.03 us -> none  [the longest x1 2.99 us: slice_softmax(): return powers / jnp.sum(powers, axis=-1, keepdims=True)]
    unnamed x57 -> x24, local copies, waits for them, and re-layouts: 6.96 us -> 12.3 us
  transfers between devices with their start and end apart: 2 -> 0, of which waited for: 2 -> 0; matrix products, arithmetic and copies ran while one was open for 2% -> 0% of each run, Pallas kernels for 0% -> 0%
where the time goes in v1:
time: 63.5 us; the launch traced here: 63.1 us
  Pallas kernels  49.5 us (78%)
  local copies, waits for them, and re-layouts  12.3 us (19%)
  between operations  1.31 us (2%)
    pallas_call x1, Pallas kernels, body(): pl.pallas_call(functools.partial(layer_kernel, token_stages, grad_stages,...  49.5 us
    unnamed x24, local copies, waits for them, and re-layouts  12.3 us

profile of v1, /device:TPU:0, one launch (start us, length us, event | category | flops | bytes accessed | tf_op | source)
XLA Modules:
  0.0 63.1 jit_solution(17249352502734804427)
XLA Ops:
  1.3 0.0 copy-start.7
  1.3 0.6 %copy-done.7 = bf16[32]{0:T(256)(128)(2,1)S(1)} copy-done((bf16[32]{0:T(256)(128)(2,1)S(1)}, bf16[32]{0:T(256)(128)(2,1)}, u32[]{:S(2)}) %copy-start.7) | copy-done | bytes 88
  1.9 0.0 copy-start
  1.9 1.0 %copy-done = bf16[1024,256]{1,0:T(8,128)(2,1)S(1)} copy-done((bf16[1024,256]{1,0:T(8,128)(2,1)S(1)}, bf16[1024,256]{1,0:T(8,128)(2,1)}, u32[]{:S(2)}) %copy-start) | copy-done | bytes 524312
  3.0 0.0 copy-start.1
  3.0 1.0 %copy-done.1 = bf16[1024,256]{1,0:T(8,128)(2,1)S(1)} copy-done((bf16[1024,256]{1,0:T(8,128)(2,1)S(1)}, bf16[1024,256]{1,0:T(8,128)(2,1)}, u32[]{:S(2)}) %copy-start.1) | copy-done | bytes 524312
  4.0 0.0 copy-start.2
  4.0 0.9 %copy-done.2 = bf16[256,256]{1,0:T(8,128)(2,1)S(1)} copy-done((bf16[256,256]{1,0:T(8,128)(2,1)S(1)}, bf16[256,256]{1,0:T(8,128)(2,1)}, u32[]{:S(2)}) %copy-start.2) | copy-done | bytes 131096
  4.9 0.0 copy-start.3
  4.9 0.9 %copy-done.3 = bf16[256,256]{1,0:T(8,128)(2,1)S(1)} copy-done((bf16[256,256]{1,0:T(8,128)(2,1)S(1)}, bf16[256,256]{1,0:T(8,128)(2,1)}, u32[]{:S(2)}) %copy-start.3) | copy-done | bytes 131096
  5.8 0.0 copy-start.4
  5.8 0.9 %copy-done.4 = bf16[256,256]{1,0:T(8,128)(2,1)S(1)} copy-done((bf16[256,256]{1,0:T(8,128)(2,1)S(1)}, bf16[256,256]{1,0:T(8,128)(2,1)}, u32[]{:S(2)}) %copy-start.4) | copy-done | bytes 131096
  6.7 0.0 copy-start.5
  6.7 0.7 %copy-done.5 = bf16[3,32,32]{2,1,0:T(8,128)(2,1)S(1)} copy-done((bf16[3,32,32]{2,1,0:T(8,128)(2,1)S(1)}, bf16[3,32,32]{2,1,0:T(8,128)(2,1)}, u32[]{:S(2)}) %copy-start.5) | copy-done | bytes 6168
  7.5 0.7 %copy-done.6 = bf16[32,64]{1,0:T(8,128)(2,1)S(1)} copy-done((bf16[32,64]{1,0:T(8,128)(2,1)S(1)}, bf16[32,64]{1,0:T(8,128)(2,1)}, u32[]{:S(2)}) %copy-start.6) | copy-done | bytes 4120
  8.2 49.5 %shard_map.152 = (bf16[1024,256]{1,0:T(8,128)(2,1)S(1)}, bf16[1024,256]{1,0:T(8,128)(2,1)S(1)}, f32[256,256]{1,0:T(8,128)S(1)}, f32[256,256]{1,0:T(8,128)S(1)}, ...) custom-call(s32[1]{0:T(128)S(6)} %copy.25.counts_ref, ...), custom_call_target="tpu_custom_call" | custom-call | tf_op jit(solution)/shard_map/pallas_call | solution.py:504
  57.7 0.8 %copy.26 = bf16[1024,256]{1,0:T(8,128)(2,1)} copy(bf16[1024,256]{1,0:T(8,128)(2,1)S(1)} %get-tuple-element.32) | data formatting | bytes 1048576
  58.4 0.8 %copy.27 = bf16[1024,256]{1,0:T(8,128)(2,1)} copy(bf16[1024,256]{1,0:T(8,128)(2,1)S(1)} %get-tuple-element.33) | data formatting | bytes 1048576
  59.2 0.7 %copy.28 = f32[256,256]{1,0:T(8,128)} copy(f32[256,256]{1,0:T(8,128)S(1)} %get-tuple-element.34) | data formatting | bytes 524288
  59.9 0.7 %copy.29 = f32[256,256]{1,0:T(8,128)} copy(f32[256,256]{1,0:T(8,128)S(1)} %get-tuple-element.35) | data formatting | bytes 524288
  60.6 0.6 copy.30
  61.3 0.5 copy.31
  61.8 0.6 copy.32
  62.4 0.7 %copy.33 = f32[256,256]{1,0:T(8,128)} copy(f32[256,256]{1,0:T(8,128)S(1)} %get-tuple-element.39) | data formatting | bytes 524288
  (1 shorter events, 0.0 us)
Async XLA Ops:
  1.3 0.7 %copy-start.7 = (bf16[32]{0:T(256)(128)(2,1)S(1)}, bf16[32]{0:T(256)(128)(2,1)}, u32[]{:S(2)}) copy-start(bf16[32]{0:T(256)(128)(2,1)} %param.14) | copy-start | bytes 196
  1.9 1.0 %copy-start = (bf16[1024,256]{1,0:T(8,128)(2,1)S(1)}, bf16[1024,256]{1,0:T(8,128)(2,1)}, u32[]{:S(2)}) copy-start(bf16[1024,256]{1,0:T(8,128)(2,1)} %cells_ref.1) | copy-start | bytes 1572868
  3.0 1.0 %copy-start.1 = (bf16[1024,256]{1,0:T(8,128)(2,1)S(1)}, bf16[1024,256]{1,0:T(8,128)(2,1)}, u32[]{:S(2)}) copy-start(bf16[1024,256]{1,0:T(8,128)(2,1)} %cot_ref.1) | copy-start | bytes 1572868
  4.0 0.9 %copy-start.2 = (bf16[256,256]{1,0:T(8,128)(2,1)S(1)}, bf16[256,256]{1,0:T(8,128)(2,1)}, u32[]{:S(2)}) copy-start(bf16[256,256]{1,0:T(8,128)(2,1)} %wx_ref.1) | copy-start | bytes 393220
  4.9 0.9 %copy-start.3 = (bf16[256,256]{1,0:T(8,128)(2,1)S(1)}, bf16[256,256]{1,0:T(8,128)(2,1)}, u32[]{:S(2)}) copy-start(bf16[256,256]{1,0:T(8,128)(2,1)} %wfx_ref.1) | copy-start | bytes 393220
  5.8 0.9 %copy-start.4 = (bf16[256,256]{1,0:T(8,128)(2,1)S(1)}, bf16[256,256]{1,0:T(8,128)(2,1)}, u32[]{:S(2)}) copy-start(bf16[256,256]{1,0:T(8,128)(2,1)} %wout_ref.1) | copy-start | bytes 393220
  6.7 0.7 %copy-start.5 = (bf16[3,32,32]{2,1,0:T(8,128)(2,1)S(1)}, bf16[3,32,32]{2,1,0:T(8,128)(2,1)}, u32[]{:S(2)}) copy-start(bf16[3,32,32]{2,1,0:T(8,128)(2,1)} %wqkv_ref.1) | copy-start | bytes 18436
  7.5 0.7 %copy-start.6 = (bf16[32,64]{1,0:T(8,128)(2,1)S(1)}, bf16[32,64]{1,0:T(8,128)(2,1)}, u32[]{:S(2)}) copy-start(bf16[32,64]{1,0:T(8,128)(2,1)} %wslice_ref.1) | copy-start | bytes 12292

commit v2 on v1

v2 whole, which is shorter than its diff:
```python
import functools
import math

import jax
import jax.numpy as jnp
from jax import lax
from jax.experimental import pallas as pl
from jax.experimental.pallas import tpu as pltpu
from jax.sharding import PartitionSpec as P

HEAD = 32
SLICES = 64
HEADS = 8
WIDTH = HEAD * HEADS
SPREAD = SLICES * HEADS
HALF = WIDTH // 2
CHUNK = 256
F32 = jnp.float32
BF16 = jnp.bfloat16
MESH = pl.DeviceIdType.MESH


def mm(left, right):
    return jnp.dot(left, right, preferred_element_type=F32)


def mm_nt(left, right):
    return lax.dot_general(left, right, (((1,), (1,)), ((), ())), preferred_element_type=F32)


def mm_tn(left, right):
    return lax.dot_general(left, right, (((0,), (0,)), ((), ())), preferred_element_type=F32)


def split(value):
    high = value.astype(BF16)
    return high, (value - high.astype(F32)).astype(BF16)


def pick2(value, ones):
    high, low = split(value)
    return mm(high, ones) + mm(low, ones)


def pick3(value, ones, product=mm):
    high = value.astype(BF16)
    rest = value - high.astype(F32)
    middle, low = split(rest)
    return product(high, ones) + product(middle, ones) + product(low, ones)


def wide(left, right, product):
    left_high, left_low = split(left)
    right_high, right_low = split(right)
    return (
        product(left_high, right_high)
        + product(left_high, right_low)
        + product(left_low, right_high)
    )


def block_mask(shape, row_width, column_width):
    rows = lax.broadcasted_iota(jnp.int32, shape, 0)
    columns = lax.broadcasted_iota(jnp.int32, shape, 1)
    return (rows // row_width) == (columns // column_width)


def stages_of(devices, rows, tile):
    sizes, rest = [2], devices // 2
    while rest > 1:
        size = min(8, rest)
        sizes.append(size)
        rest //= size
    stages, stride = [], 1
    for size in sizes:
        scattered = rows % (size * tile) == 0
        stages.append((size, stride, rows, scattered))
        rows = rows // size if scattered else rows
        stride *= size
    return stages


def peers_of(stage):
    size, stride, _, _ = stage
    me = lax.axis_index("dom")
    place = lax.rem(lax.div(me, stride), size)
    others = []
    for step in range(1, size):
        there = lax.rem(place + step, size)
        others.append((there, me + (there - place) * stride))
    return place, others


class Reduction:
    @staticmethod
    def scratch(stages, columns, dtype):
        shapes = []
        for size, _, rows, scattered in stages:
            part = rows // size if scattered else rows
            shapes += [
                pltpu.VMEM((rows, columns), dtype),
                pltpu.VMEM((size, part, columns), dtype),
                pltpu.VMEM((rows, columns), dtype),
                pltpu.SemaphoreType.DMA((4, size)),
            ]
        return shapes

    def __init__(self, stages, refs):
        self.stages = stages
        self.levels = [refs[4 * i : 4 * i + 4] for i in range(len(stages))]

    def source(self):
        return self.levels[0][0]

    def total(self):
        return self.levels[0][2]

    def send(self, index):
        stage = self.stages[index]
        size, _, rows, scattered = stage
        source, received, _, sems = self.levels[index]
        place, others = peers_of(stage)
        part = rows // size if scattered else rows
        self.flying = []
        for step, (there, device) in enumerate(others):
            cut = source
            if scattered:
                cut = source.at[pl.ds(pl.multiple_of(there * part, part), part), :]
            copy = pltpu.make_async_remote_copy(
                src_ref=cut,
                dst_ref=received.at[place],
                send_sem=sems.at[0, step],
                recv_sem=sems.at[1, step],
                device_id={"dom": device},
                device_id_type=MESH,
            )
            copy.start()
            self.flying.append(copy)
        if scattered:
            received[place] = source[pl.ds(pl.multiple_of(place * part, part), part), :]
        else:
            received[place] = source[...]

    def fold(self, index):
        size, _, rows, scattered = self.stages[index]
        source, received, gathered, _ = self.levels[index]
        for copy in self.flying:
            copy.wait()
        total = received[0].astype(F32)
        for slot in range(1, size):
            total = total + received[slot].astype(F32)
        total = total.astype(source.dtype)
        if index + 1 < len(self.stages):
            self.levels[index + 1][0][...] = total
        else:
            self.place(index, total)

    def place(self, index, value):
        size, _, rows, scattered = self.stages[index]
        gathered = self.levels[index][2]
        if scattered:
            part = rows // size
            place, _ = peers_of(self.stages[index])
            gathered[pl.ds(pl.multiple_of(place * part, part), part), :] = value
        else:
            gathered[...] = value

    def gather(self, index):
        stage = self.stages[index]
        size, _, rows, scattered = stage
        gathered, sems = self.levels[index][2:]
        self.flying = []
        if not scattered:
            return
        part = rows // size
        place, others = peers_of(stage)
        mine = gathered.at[pl.ds(pl.multiple_of(place * part, part), part), :]
        for step, (_, device) in enumerate(others):
            copy = pltpu.make_async_remote_copy(
                src_ref=mine,
                dst_ref=mine,
                send_sem=sems.at[2, step],
                recv_sem=sems.at[3, step],
                device_id={"dom": device},
                device_id_type=MESH,
            )
            copy.start()
            self.flying.append(copy)

    def settle(self, index):
        for copy in self.flying:
            copy.wait()
        if index > 0:
            self.place(index - 1, self.levels[index][2][...])

    def last(self):
        return len(self.stages) - 1


def layer_kernel(
    token_stages,
    grad_stages,
    scale,
    counts_hbm,
    cells_hbm,
    cot_hbm,
    wx_hbm,
    wfx_hbm,
    wslice_hbm,
    wtemp_hbm,
    wqkv_hbm,
    wout_hbm,
    result_hbm,
    gcells_hbm,
    gwx_hbm,
    gwfx_hbm,
    gslice_hbm,
    gtemp_hbm,
    gqkv_hbm,
    gout_hbm,
    counts_ref,
    cells_ref,
    cot_ref,
    wx_ref,
    wfx_ref,
    wslice_ref,
    wtemp_ref,
    wqkv_ref,
    wout_ref,
    result_ref,
    gcells_ref,
    gwx_ref,
    gwfx_ref,
    gslice_ref,
    gtemp_ref,
    gqkv_ref,
    gout_ref,
    in_sems,
    out_sems,
    proj_ref,
    pair_ref,
    weight_ref,
    prob_ref,
    slope_ref,
    scaled_ref,
    inverse_ref,
    sigmoid_ref,
    cells_t,
    cot_t,
    proj_t,
    hidden_ref,
    dfeat_ref,
    dproj_ref,
    dlogit_ref,
    dtemp_ref,
    slice_bd,
    temp_bd,
    temp_row,
    same_head,
    maps_ref,
    acc_tokens,
    both_bd,
    *sum_refs,
):
    rows = cells_ref.shape[0]
    chunks = rows // CHUNK
    middle = chunks // 2
    levels = 4 * len(token_stages)
    levels_g = 4 * len(grad_stages)
    token_sum = Reduction(token_stages, sum_refs[:levels])
    early_sum, late_sum, last_sum = [
        Reduction(grad_stages, sum_refs[levels + i * levels_g : levels + (i + 1) * levels_g])
        for i in range(3)
    ]

    pairs = (
        (wslice_hbm, wslice_ref),
        (wtemp_hbm, wtemp_ref),
        (cells_hbm, cells_ref),
        (wx_hbm, wx_ref),
        (counts_hbm, counts_ref),
        (wfx_hbm, wfx_ref),
        (wout_hbm, wout_ref),
        (cot_hbm, cot_ref),
        (wqkv_hbm, wqkv_ref),
    )
    incoming = [
        pltpu.make_async_copy(there, here, in_sems.at[i]) for i, (there, here) in enumerate(pairs)
    ]
    for copy in incoming:
        copy.start()
    barrier = pltpu.get_barrier_semaphore()
    greeted = 0
    for stage in token_stages:
        for _, device in peers_of(stage)[1]:
            pl.semaphore_signal(barrier, inc=1, device_id={"dom": device}, device_id_type=MESH)
            greeted += 1
    outgoing = []

    def put(source, target):
        copy = pltpu.make_async_copy(source, target, out_sems.at[len(outgoing)])
        copy.start()
        outgoing.append(copy)

    repeat32 = (
        (lax.broadcasted_iota(jnp.int32, (HEAD, HALF), 1) % HEAD)
        == lax.broadcasted_iota(jnp.int32, (HEAD, HALF), 0)
    ).astype(BF16)
    repeat64 = (
        (lax.broadcasted_iota(jnp.int32, (SLICES, 256), 1) % SLICES)
        == lax.broadcasted_iota(jnp.int32, (SLICES, 256), 0)
    ).astype(BF16)
    lane_head = lax.broadcasted_iota(jnp.int32, (256, 128), 1)
    row_head = lax.broadcasted_iota(jnp.int32, (256, 128), 0) // SLICES
    gather_heads = [(row_head + 4 * half == lane_head).astype(BF16) for half in range(2)]
    spread_lane = lax.broadcasted_iota(jnp.int32, (128, 256), 1) // SLICES
    spread_row = lax.broadcasted_iota(jnp.int32, (128, 256), 0)
    spread_heads = [(spread_lane + 4 * half == spread_row).astype(BF16) for half in range(2)]
    half_diag = block_mask((256, HALF), SLICES, HEAD)
    same_head[...] = block_mask((256, 256), SLICES, SLICES).astype(BF16)

    incoming[0].wait()
    incoming[1].wait()
    tall = mm_tn(repeat32, wslice_ref[...]).astype(BF16)
    slice_bd[...] = jnp.where(
        block_mask((HALF, 256), HEAD, SLICES), mm(tall, repeat64), 0.0
    ).astype(BF16)
    temp_rows = jnp.broadcast_to(wtemp_ref[...], (128, HEAD))
    column = mm_nt(repeat32.T, temp_rows)
    line = mm(temp_rows, repeat32)
    for half in range(2):
        place = slice(half * HALF, (half + 1) * HALF)
        lanes = lax.broadcasted_iota(jnp.int32, (HALF, 128), 1)
        heads = lax.broadcasted_iota(jnp.int32, (HALF, 128), 0) // HEAD + 4 * half
        temp_bd[place, :] = jnp.where(lanes == heads, column, 0.0).astype(BF16)
        heads = lax.broadcasted_iota(jnp.int32, (128, HALF), 1) // HEAD + 4 * half
        here = lax.broadcasted_iota(jnp.int32, (128, HALF), 0)
        temp_row[:, place] = jnp.where(here == heads, line, 0.0).astype(BF16)
    acc_tokens[...] = jnp.zeros_like(acc_tokens)
    for copy in incoming[2:]:
        copy.wait()
    count = counts_ref[0]

    def cut(index):
        return pl.ds(pl.multiple_of(index * CHUNK, CHUNK), CHUNK)

    def forward(index, carry):
        part = cut(index)
        cells = cells_ref[part, :]
        projected = mm(cells, wx_ref[...]).astype(BF16)
        features = mm(cells, wfx_ref[...]).astype(BF16)
        d_hidden = mm_nt(cot_ref[part, :], wout_ref[...]).astype(BF16)
        temp_lin = mm(projected, temp_bd[...])
        away = jnp.exp(-jnp.abs(temp_lin))
        temper = 0.5 + (jnp.maximum(temp_lin, 0.0) + jnp.log(1.0 + away))
        inverse = 1.0 / temper
        sigmoid = jnp.where(temp_lin >= 0.0, 1.0, away) / (1.0 + away)
        proj_ref[part, :] = projected
        inverse_ref[part, :] = inverse
        sigmoid_ref[part, :] = sigmoid
        inverse_high, inverse_low = split(inverse)
        place = lax.broadcasted_iota(jnp.int32, (CHUNK, 1), 0) + index * CHUNK
        live = (place < count).astype(F32)
        for half in range(2):
            lanes = slice(half * HALF, (half + 1) * HALF)
            span = slice(half * 256, (half + 1) * 256)
            bent = jnp.tanh(mm(projected[:, lanes], slice_bd[...]) / 10.0)
            cool = mm(inverse_high, spread_heads[half]) + mm(inverse_low, spread_heads[half])
            scaled = (10.0 * bent) * cool
            powers = jnp.exp(scaled)
            probs = powers * (live / pick2(powers, same_head[...]))
            weights = probs.astype(BF16)
            weight_ref[part, span] = weights
            prob_ref[part, span] = probs
            slope_ref[part, span] = (1.0 - bent * bent) * cool
            scaled_ref[part, span] = scaled
            pair = jnp.concatenate([d_hidden[:, lanes], features[:, lanes]], axis=1)
            pair_ref[part, span] = pair
            right = jnp.concatenate([pair, jnp.ones((CHUNK, 128), BF16)], axis=1)
            acc_tokens[half] += mm_tn(weights, right)
        return carry

    lax.fori_loop(0, chunks, forward, 0)

    payload = token_sum.source()
    lane = lax.broadcasted_iota(jnp.int32, (SLICES, 128), 1)
    totals = jnp.zeros((SLICES, 128), F32)
    for half in range(2):
        lanes = slice(half * HALF, (half + 1) * HALF)
        dmix = jnp.where(half_diag, acc_tokens[half, :, 0:HALF], 0.0)
        numer = jnp.where(half_diag, acc_tokens[half, :, HALF : 2 * HALF], 0.0)
        payload[0:SLICES, lanes] = sum(numer[i * 64 : i * 64 + 64] for i in range(4))
        payload[SLICES : 2 * SLICES, lanes] = sum(dmix[i * 64 : i * 64 + 64] for i in range(4))
        for i in range(4):
            block = acc_tokens[half, i * 64 : i * 64 + 64, 2 * HALF : 2 * HALF + 128]
            totals = totals + jnp.where(lane == half * 4 + i, block, 0.0)
    payload[0:SLICES, WIDTH : WIDTH + 128] = totals
    payload[SLICES : 2 * SLICES, WIDTH : WIDTH + 128] = jnp.zeros((SLICES, 128), F32)

    pl.semaphore_wait(barrier, greeted)
    diag_square = block_mask((WIDTH, WIDTH), HEAD, HEAD)

    def prepare_maps():
        for k in range(3):
            square = mm(mm_tn(repeat32, wqkv_ref[k]).astype(BF16), repeat32)
            square = jnp.concatenate([square, square], axis=0)
            square = jnp.concatenate([square, square], axis=1)
            maps_ref[k] = jnp.where(diag_square, square, 0.0).astype(BF16)

    def turn(source, target):
        for index in range(chunks):
            part = slice(index * CHUNK, (index + 1) * CHUNK)
            target[:, part] = source[part, :].T

    fillers = [
        prepare_maps,
        functools.partial(turn, cells_ref, cells_t),
        functools.partial(turn, cot_ref, cot_t),
        functools.partial(turn, proj_ref, proj_t),
    ]
    for index in range(len(token_stages)):
        token_sum.send(index)
        if fillers:
            fillers.pop(0)()
        token_sum.fold(index)
    for index in reversed(range(len(token_stages))):
        token_sum.gather(index)
        if fillers:
            fillers.pop(0)()
        token_sum.settle(index)
    for filler in fillers:
        filler()

    total = token_sum.total()
    numerators = total[0:SLICES, 0:WIDTH]
    d_mixed = total[SLICES : 2 * SLICES, 0:WIDTH]
    spread32 = block_mask((128, WIDTH), 1, HEAD).astype(BF16)
    denominators = pick3(total[0:SLICES, WIDTH : WIDTH + 128], spread32) + 1e-05
    tokens = numerators / denominators
    queries, key_rows, value_rows = [pick2(tokens, maps_ref[k]) for k in range(3)]

    def expand(value):
        return jnp.where(half_diag, jnp.concatenate([value] * 4, axis=0), 0.0)

    def contract(value):
        value = jnp.where(half_diag, value, 0.0)
        return sum(value[i * SLICES : (i + 1) * SLICES] for i in range(4))

    root = 1.0 / math.sqrt(HEAD)
    halves = [slice(half * HALF, (half + 1) * HALF) for half in range(2)]
    keys_bd = [expand(key_rows[:, lanes]) for lanes in halves]
    values_bd = [expand(value_rows[:, lanes]) for lanes in halves]
    d_attention = [wide(d_mixed[:, halves[i]], values_bd[i], mm_nt) for i in range(2)]
    bent = [
        jnp.tanh(wide(queries[:, halves[i]], keys_bd[i], mm_nt) * root / 10.0) for i in range(2)
    ]
    powers = [jnp.exp(10.0 * value) for value in bent]
    attention = [value / pick2(value, same_head[...]) for value in powers]
    for i in range(2):
        mixed = wide(attention[i], values_bd[i], mm)
        both_bd[i, :, 0:HALF] = expand(mixed).astype(BF16)
    shared = [attention[i] * d_attention[i] for i in range(2)]
    shared = [shared[i] - attention[i] * pick2(shared[i], same_head[...]) for i in range(2)]
    d_scores = [shared[i] * (1.0 - bent[i] * bent[i]) * root for i in range(2)]
    d_queries = jnp.concatenate([wide(d_scores[i], keys_bd[i], mm) for i in range(2)], axis=1)
    d_keys = jnp.concatenate(
        [contract(wide(d_scores[i], queries[:, halves[i]], mm_tn)) for i in range(2)], axis=1
    )
    d_values = jnp.concatenate(
        [contract(wide(attention[i], d_mixed[:, halves[i]], mm_tn)) for i in range(2)], axis=1
    )
    d_maps = (d_queries, d_keys, d_values)

    def pick_back(value, weight):
        high, low = split(value)
        return mm_nt(high, weight) + mm_nt(low, weight)

    d_tokens = sum(pick_back(d_maps[k], maps_ref[k]) for k in range(3))
    d_numer = d_tokens / denominators
    away = d_numer * tokens
    d_denom = []
    for i in range(2):
        both_bd[i, :, HALF : 2 * HALF] = expand(d_numer[:, halves[i]]).astype(BF16)
        high, low = split(expand(away[:, halves[i]]))
        ones = jnp.ones((128, HALF), BF16)
        d_denom.append(-(mm_nt(ones, high) + mm_nt(ones, low))[0:1, :])

    def early(index, carry):
        part = cut(index)
        for half in range(2):
            lanes = slice(half * HALF, (half + 1) * HALF)
            made = mm(weight_ref[part, half * 256 : (half + 1) * 256], both_bd[half]).astype(BF16)
            hidden_ref[part, lanes] = made[:, 0:HALF]
            dfeat_ref[part, lanes] = made[:, HALF : 2 * HALF]
        return carry

    lax.fori_loop(0, chunks, early, 0)
    source = early_sum.source()
    source[:, 0:WIDTH] = mm(cot_t[...], hidden_ref[...]).astype(BF16)
    source[:, WIDTH : 2 * WIDTH] = mm(cells_t[...], dfeat_ref[...]).astype(BF16)

    def backward(half, index, carry):
        part = cut(index)
        lanes = slice(half * HALF, (half + 1) * HALF)
        span = slice(half * 256, (half + 1) * 256)
        d_weights = mm_nt(pair_ref[part, span], both_bd[half]) + d_denom[half]
        probs = prob_ref[part, span]
        shared = probs * d_weights
        shared = shared - probs * pick2(shared, same_head[...])
        d_logits = (shared * slope_ref[part, span]).astype(BF16)
        d_temper = -pick2(shared * scaled_ref[part, span], gather_heads[half])
        d_temp = (d_temper * inverse_ref[part, :] * sigmoid_ref[part, :]).astype(BF16)
        dlogit_ref[part, :] = d_logits
        dtemp_ref[part, :] = d_temp
        dproj_ref[part, lanes] = (
            mm_nt(d_logits, slice_bd[...]) + mm(d_temp, temp_row[:, lanes])
        ).astype(BF16)
        return carry

    def fill(half, target):
        lanes = slice(half * HALF, (half + 1) * HALF)
        block = mm(proj_t[lanes, :], dlogit_ref[...])
        block = jnp.where(block_mask((HALF, 256), HEAD, SLICES), block, 0.0)
        block = block[:, 0:128] + block[:, 128:256]
        block = block + pltpu.roll(block, 64, 1)
        here = lax.broadcasted_iota(jnp.int32, (HALF, 128), 1)
        heads = lax.broadcasted_iota(jnp.int32, (HALF, 128), 0) // HEAD + 4 * half
        own = jnp.where(here == heads, mm(proj_t[lanes, :], dtemp_ref[...]), 0.0)
        own = jnp.sum(own, axis=1, keepdims=True)
        target[:, 0:128] = mm(cells_t[...], dproj_ref[:, lanes]).astype(BF16)
        target[0:HALF, 128:256] = jnp.where(here < SLICES, block, own).astype(BF16)
        target[HALF:WIDTH, 128:256] = jnp.zeros((WIDTH - HALF, 128), BF16)

    def results(index, carry):
        part = cut(index)
        result_ref[part, :] = mm(hidden_ref[part, :], wout_ref[...]).astype(BF16)
        return carry

    def cell_grads(index, carry):
        part = cut(index)
        gcells_ref[part, :] = (
            mm_nt(dproj_ref[part, :], wx_ref[...]) + mm_nt(dfeat_ref[part, :], wfx_ref[...])
        ).astype(BF16)
        return carry

    def steps(reduction):
        for index in range(len(grad_stages)):
            reduction.send(index)
            yield
            reduction.fold(index)
        for index in reversed(range(len(grad_stages))):
            reduction.gather(index)
            yield
            reduction.settle(index)

    early_steps, late_steps, last_steps = steps(early_sum), steps(late_sum), steps(last_sum)
    next(early_steps)
    lax.fori_loop(0, middle, functools.partial(backward, 0), 0)
    next(early_steps)
    lax.fori_loop(middle, chunks, functools.partial(backward, 0), 0)
    fill(0, late_sum.source())
    next(late_steps)
    next(early_steps)
    lax.fori_loop(0, middle, functools.partial(backward, 1), 0)
    next(late_steps)
    next(early_steps)
    lax.fori_loop(middle, chunks, functools.partial(backward, 1), 0)
    fill(1, last_sum.source())
    next(last_steps)
    next(late_steps)
    lax.fori_loop(0, chunks, cell_grads, 0)
    put(gcells_ref, gcells_hbm)
    next(last_steps)
    for _ in early_steps:
        pass
    lax.fori_loop(0, chunks, results, 0)
    put(result_ref, result_hbm)
    gwfx_ref[...] = early_sum.total()[:, WIDTH : 2 * WIDTH].astype(F32) * scale
    put(gwfx_ref, gwfx_hbm)
    gout_ref[...] = early_sum.total()[:, 0:WIDTH].astype(F32).T * scale
    put(gout_ref, gout_hbm)
    next(late_steps)
    for k in range(3):
        square = jnp.where(diag_square, wide(tokens, d_maps[k], mm_tn), 0.0)
        strip = sum(square[i * HEAD : (i + 1) * HEAD] for i in range(HEADS))
        strip = strip[:, 0:HALF] + strip[:, HALF:WIDTH]
        gqkv_ref[k] = pick2(strip, repeat32.T) * scale
    put(gqkv_ref, gqkv_hbm)
    next(last_steps)
    for _ in late_steps:
        pass
    gwx_ref[:, 0:HALF] = late_sum.total()[:, 0:HALF].astype(F32) * scale
    for _ in last_steps:
        pass
    gwx_ref[:, HALF:WIDTH] = last_sum.total()[:, 0:HALF].astype(F32) * scale
    put(gwx_ref, gwx_hbm)
    extra = sum(
        reduction.total()[0:HALF, 128:256].astype(F32) for reduction in (late_sum, last_sum)
    )
    extra = sum(extra[i * HEAD : (i + 1) * HEAD] for i in range(4)) * scale
    gslice_ref[...] = extra[:, 0:SLICES]
    put(gslice_ref, gslice_hbm)
    unit = (
        lax.broadcasted_iota(jnp.int32, (HEAD, HEAD), 0)
        == lax.broadcasted_iota(jnp.int32, (HEAD, HEAD), 1)
    ).astype(BF16)
    gtemp_ref[...] = pick3(extra, unit, mm_tn)[SLICES : SLICES + 1, :]
    put(gtemp_ref, gtemp_hbm)
    for copy in outgoing:
        copy.wait()


def hand_over(*refs):
    count = (len(refs) - 1) // 2
    copies = [
        pltpu.make_async_copy(refs[i], refs[count + i], refs[-1].at[i]) for i in range(count)
    ]
    for copy in copies:
        copy.start()
    for copy in copies:
        copy.wait()


def body(devices, cells, counts, w_x, w_fx, w_slice, w_temp, w_qkv, w_out, cotangent):
    rows = cells.shape[0]
    token_stages = stages_of(devices, 2 * SLICES, 8)
    grad_stages = stages_of(devices, WIDTH, 16)
    scale = 1.0 / math.sqrt(rows * devices)
    anywhere = pl.BlockSpec(memory_space=pl.ANY)
    vmem = pltpu.VMEM
    out_shapes = [
        ((rows, WIDTH), BF16),
        ((rows, WIDTH), BF16),
        ((WIDTH, WIDTH), F32),
        ((WIDTH, WIDTH), F32),
        ((HEAD, SLICES), F32),
        ((1, HEAD), F32),
        ((3, HEAD, HEAD), F32),
        ((WIDTH, WIDTH), F32),
    ]
    out_shape = tuple(jax.ShapeDtypeStruct(*one) for one in out_shapes)
    outs = pl.pallas_call(
        functools.partial(layer_kernel, token_stages, grad_stages, scale),
        out_shape=out_shape,
        in_specs=[anywhere] * 9,
        out_specs=[anywhere] * 8,
        scratch_shapes=[
            pltpu.SMEM((1,), jnp.int32),
            vmem((rows, WIDTH), BF16),
            vmem((rows, WIDTH), BF16),
            vmem((WIDTH, WIDTH), BF16),
            vmem((WIDTH, WIDTH), BF16),
            vmem((HEAD, SLICES), BF16),
            vmem((1, HEAD), BF16),
            vmem((3, HEAD, HEAD), BF16),
            vmem((WIDTH, WIDTH), BF16),
        ]
        + [vmem(*one) for one in out_shapes]
        + [
            pltpu.SemaphoreType.DMA((9,)),
            pltpu.SemaphoreType.DMA((8,)),
            vmem((rows, WIDTH), BF16),
            vmem((rows, SPREAD), BF16),
            vmem((rows, SPREAD), BF16),
            vmem((rows, SPREAD), F32),
            vmem((rows, SPREAD), F32),
            vmem((rows, SPREAD), F32),
            vmem((rows, 128), F32),
            vmem((rows, 128), F32),
            vmem((WIDTH, rows), BF16),
            vmem((WIDTH, rows), BF16),
            vmem((WIDTH, rows), BF16),
            vmem((rows, WIDTH), BF16),
            vmem((rows, WIDTH), BF16),
            vmem((rows, WIDTH), BF16),
            vmem((rows, 256), BF16),
            vmem((rows, 128), BF16),
            vmem((HALF, 256), BF16),
            vmem((WIDTH, 128), BF16),
            vmem((128, WIDTH), BF16),
            vmem((256, 256), BF16),
            vmem((3, WIDTH, WIDTH), BF16),
            vmem((2, 256, 2 * HALF + 128), F32),
            vmem((2, 256, 2 * HALF), BF16),
        ]
        + Reduction.scratch(token_stages, WIDTH + 128, F32)
        + Reduction.scratch(grad_stages, 2 * WIDTH, BF16)
        + Reduction.scratch(grad_stages, 256, BF16)
        + Reduction.scratch(grad_stages, 256, BF16),
        compiler_params=pltpu.CompilerParams(
            collective_id=0, has_side_effects=True, vmem_limit_bytes=60 * 1024 * 1024
        ),
    )(counts, cells, cotangent, w_x, w_fx, w_slice, w_temp.reshape(1, HEAD), w_qkv, w_out)
    outs = pl.pallas_call(
        hand_over,
        out_shape=out_shape,
        in_specs=[anywhere] * 8,
        out_specs=[anywhere] * 8,
        scratch_shapes=[pltpu.SemaphoreType.DMA((8,))],
        compiler_params=pltpu.CompilerParams(vmem_limit_bytes=60 * 1024 * 1024),
    )(*outs)
    result, gcells, gwx, gwfx, gslice, gtemp, gqkv, gout = outs
    return result, gcells, gwx, gwfx, gslice, gtemp.reshape(HEAD), gqkv, gout


def solution(mesh):
    placed = (
        P(("groups", "dom"), None),
        P(("groups", "dom")),
        P(),
        P(),
        P(),
        P(),
        P(),
        P(),
        P(("groups", "dom"), None),
    )
    return jax.shard_map(
        functools.partial(body, mesh.shape["dom"]),
        mesh=mesh,
        in_specs=placed,
        out_specs=(
            P(("groups", "dom"), None),
            P(("groups", "dom"), None),
            P("groups", None),
            P("groups", None),
            P("groups", None),
            P("groups"),
            P("groups", None, None),
            P("groups", None),
        ),
        check_vma=False,
    )
```

time: 63.5 us -> 113 us (1.78)
  Pallas kernels: 49.5 us -> 112 us
  local copies, waits for them, and re-layouts: 12.3 us -> 0 us
    pallas_call x0 -> x1, Pallas kernels: none -> 58.8 us  [body(): pl.pallas_call(hand_over, out_shape=out_shape, in_specs=[anywhere] * 8, o...]
    unnamed x24 -> x0, local copies, waits for them, and re-layouts: 12.3 us -> none
    pallas_call x1, Pallas kernels: 49.5 us -> 53.1 us  [body(): pl.pallas_call(functools.partial(layer_kernel, token_stages, grad_stages,...]
where the time goes in v2:
time: 113 us
  Pallas kernels  112 us (99%)
  between operations  1.29 us (1%)
    pallas_call x1, Pallas kernels, body(): pl.pallas_call(hand_over, out_shape=out_shape, in_specs=[anywhere] * 8, o...  58.8 us
    pallas_call x1, Pallas kernels, body(): pl.pallas_call(functools.partial(layer_kernel, token_stages, grad_stages,...  53.1 us

profile of v2, /device:TPU:0, one launch (start us, length us, event | category | flops | bytes accessed | tf_op | source)
XLA Modules:
  0.0 113.2 jit_solution(2453246058183971675)
XLA Ops:
  1.3 53.1 %shard_map.152 = (bf16[1024,256]{1,0:T(8,128)(2,1)}, bf16[1024,256]{1,0:T(8,128)(2,1)}, f32[256,256]{1,0:T(8,128)}, f32[256,256]{1,0:T(8,128)}, f32[32,64]{1,0:T...) custom-call(s32[1]{0:T(128)S(6)} %copy.17.counts_hbm, bf16[1024,256]{1,0:T(8,128)(2,1)} %cells_hbm.1, ...), custom_call_target="tpu_custom_call" | custom-call | tf_op jit(solution)/shard_map/pallas_call | solution.py:642
  54.4 58.8 %shard_map.153 = (bf16[1024,256]{1,0:T(8,128)(2,1)}, bf16[1024,256]{1,0:T(8,128)(2,1)}, f32[256,256]{1,0:T(8,128)}, f32[256,256]{1,0:T(8,128)}, f32[32,64]{1,0:T...) custom-call(bf16[1024,256]{1,0:T(8,128)(2,1)} %get-tuple-element.24.refs_0_, ...), custom_call_target="tpu_custom_call" | custom-call | tf_op jit(solution)/shard_map/pallas_call | solution.py:694

commit v3 on v2

--- a/solution.py
+++ b/solution.py
@@ -260,6 +260,11 @@
     maps_ref,
     acc_tokens,
     both_bd,
+    both_t,
+    slice_t,
+    wout_t,
+    wx_t,
+    wfx_t,
     *sum_refs,
 ):
     rows = cells_ref.shape[0]
@@ -339,6 +344,7 @@
     acc_tokens[...] = jnp.zeros_like(acc_tokens)
     for copy in incoming[2:]:
         copy.wait()
+    wout_t[...] = wout_ref[...].T
     count = counts_ref[0]
 
     def cut(index):
@@ -349,7 +355,7 @@
         cells = cells_ref[part, :]
         projected = mm(cells, wx_ref[...]).astype(BF16)
         features = mm(cells, wfx_ref[...]).astype(BF16)
-        d_hidden = mm_nt(cot_ref[part, :], wout_ref[...]).astype(BF16)
+        d_hidden = mm(cot_ref[part, :], wout_t[...]).astype(BF16)
         temp_lin = mm(projected, temp_bd[...])
         away = jnp.exp(-jnp.abs(temp_lin))
         temper = 0.5 + (jnp.maximum(temp_lin, 0.0) + jnp.log(1.0 + away))
@@ -364,11 +370,14 @@
         for half in range(2):
             lanes = slice(half * HALF, (half + 1) * HALF)
             span = slice(half * 256, (half + 1) * 256)
-            bent = jnp.tanh(mm(projected[:, lanes], slice_bd[...]) / 10.0)
+            bent = jnp.tanh(mm(projected[:, lanes], slice_bd[...]) * 0.1)
             cool = mm(inverse_high, spread_heads[half]) + mm(inverse_low, spread_heads[half])
             scaled = (10.0 * bent) * cool
             powers = jnp.exp(scaled)
-            probs = powers * (live / pick2(powers, same_head[...]))
+            sums = pick2(powers, same_head[...])
+            over = pl.reciprocal(sums, approx=True)
+            over = over * (2.0 - sums * over)
+            probs = powers * (live * over)
             weights = probs.astype(BF16)
             weight_ref[part, span] = weights
             prob_ref[part, span] = probs
@@ -406,6 +415,9 @@
             square = jnp.concatenate([square, square], axis=0)
             square = jnp.concatenate([square, square], axis=1)
             maps_ref[k] = jnp.where(diag_square, square, 0.0).astype(BF16)
+        slice_t[...] = slice_bd[...].T
+        wx_t[...] = wx_ref[...].T
+        wfx_t[...] = wfx_ref[...].T
 
     def turn(source, target):
         for index in range(chunks):
@@ -485,6 +497,9 @@
         ones = jnp.ones((128, HALF), BF16)
         d_denom.append(-(mm_nt(ones, high) + mm_nt(ones, low))[0:1, :])
 
+    for half in range(2):
+        both_t[half] = both_bd[half].T
+
     def early(index, carry):
         part = cut(index)
         for half in range(2):
@@ -503,7 +518,7 @@
         part = cut(index)
         lanes = slice(half * HALF, (half + 1) * HALF)
         span = slice(half * 256, (half + 1) * 256)
-        d_weights = mm_nt(pair_ref[part, span], both_bd[half]) + d_denom[half]
+        d_weights = mm(pair_ref[part, span], both_t[half]) + d_denom[half]
         probs = prob_ref[part, span]
         shared = probs * d_weights
         shared = shared - probs * pick2(shared, same_head[...])
@@ -513,7 +528,7 @@
         dlogit_ref[part, :] = d_logits
         dtemp_ref[part, :] = d_temp
         dproj_ref[part, lanes] = (
-            mm_nt(d_logits, slice_bd[...]) + mm(d_temp, temp_row[:, lanes])
+            mm(d_logits, slice_t[...]) + mm(d_temp, temp_row[:, lanes])
         ).astype(BF16)
         return carry
 
@@ -539,7 +554,7 @@
     def cell_grads(index, carry):
         part = cut(index)
         gcells_ref[part, :] = (
-            mm_nt(dproj_ref[part, :], wx_ref[...]) + mm_nt(dfeat_ref[part, :], wfx_ref[...])
+            mm(dproj_ref[part, :], wx_t[...]) + mm(dfeat_ref[part, :], wfx_t[...])
         ).astype(BF16)
         return carry
 
@@ -611,13 +626,18 @@
 
 
 def hand_over(*refs):
-    count = (len(refs) - 1) // 2
-    copies = [
-        pltpu.make_async_copy(refs[i], refs[count + i], refs[-1].at[i]) for i in range(count)
-    ]
+    count = (len(refs) - 2) // 3
+    sources, targets, between = refs[:count], refs[count : 2 * count], refs[2 * count : 3 * count]
+    arrive, leave = refs[-2:]
+    copies = [pltpu.make_async_copy(sources[i], between[i], arrive.at[i]) for i in range(count)]
     for copy in copies:
         copy.start()
-    for copy in copies:
+    onward = []
+    for i, copy in enumerate(copies):
+        copy.wait()
+        onward.append(pltpu.make_async_copy(between[i], targets[i], leave.at[i]))
+        onward[-1].start()
+    for copy in onward:
         copy.wait()
 
 
@@ -682,6 +702,11 @@
             vmem((3, WIDTH, WIDTH), BF16),
             vmem((2, 256, 2 * HALF + 128), F32),
             vmem((2, 256, 2 * HALF), BF16),
+            vmem((2, 256, 2 * HALF), BF16),
+            vmem((256, HALF), BF16),
+            vmem((WIDTH, WIDTH), BF16),
+            vmem((WIDTH, WIDTH), BF16),
+            vmem((WIDTH, WIDTH), BF16),
         ]
         + Reduction.scratch(token_stages, WIDTH + 128, F32)
         + Reduction.scratch(grad_stages, 2 * WIDTH, BF16)
@@ -696,7 +721,7 @@
         out_shape=out_shape,
         in_specs=[anywhere] * 8,
         out_specs=[anywhere] * 8,
-        scratch_shapes=[pltpu.SemaphoreType.DMA((8,))],
+        scratch_shapes=[vmem(*one) for one in out_shapes] + [pltpu.SemaphoreType.DMA((8,))] * 2,
         compiler_params=pltpu.CompilerParams(vmem_limit_bytes=60 * 1024 * 1024),
     )(*outs)
     result, gcells, gwx, gwfx, gslice, gtemp, gqkv, gout = outs

time: 113 us -> 57.1 us (0.51)
  Pallas kernels: 112 us -> 55.6 us
    pallas_call x1, Pallas kernels: 58.8 us -> 2.43 us  [body(): pl.pallas_call(hand_over, out_shape=out_shape, in_specs=[anywhere] * 8, o...]
where the time goes in v3:
time: 57.1 us; the launch traced here: 56.8 us
  Pallas kernels  55.6 us (97%)
  between operations  1.29 us (2%)
    pallas_call x1, Pallas kernels, body(): pl.pallas_call(functools.partial(layer_kernel, token_stages, grad_stages,...  53.1 us
    pallas_call x1, Pallas kernels, body(): pl.pallas_call(hand_over, out_shape=out_shape, in_specs=[anywhere] * 8, o...  2.43 us

profile of v3, /device:TPU:0, one launch (start us, length us, event | category | flops | bytes accessed | tf_op | source)
XLA Modules:
  0.0 56.8 jit_solution(11300250849355846681)
XLA Ops:
  1.3 53.1 %shard_map.152 = (bf16[1024,256]{1,0:T(8,128)(2,1)}, bf16[1024,256]{1,0:T(8,128)(2,1)}, f32[256,256]{1,0:T(8,128)}, f32[256,256]{1,0:T(8,128)}, f32[32,64]{1,0:T...) custom-call(s32[1]{0:T(128)S(6)} %copy.17.counts_hbm, bf16[1024,256]{1,0:T(8,128)(2,1)} %cells_hbm.1, ...), custom_call_target="tpu_custom_call" | custom-call | tf_op jit(solution)/shard_map/pallas_call | solution.py:662
  54.4 2.4 %shard_map.153 = (bf16[1024,256]{1,0:T(8,128)(2,1)}, bf16[1024,256]{1,0:T(8,128)(2,1)}, f32[256,256]{1,0:T(8,128)}, f32[256,256]{1,0:T(8,128)}, f32[32,64]{1,0:T...) custom-call(bf16[1024,256]{1,0:T(8,128)(2,1)} %get-tuple-element.24.refs_0_, ...), custom_call_target="tpu_custom_call" | custom-call | tf_op jit(solution)/shard_map/pallas_call | solution.py:719

commit v4 on v3

--- a/solution.py
+++ b/solution.py
@@ -272,10 +272,12 @@
     middle = chunks // 2
     levels = 4 * len(token_stages)
     levels_g = 4 * len(grad_stages)
-    token_sum = Reduction(token_stages, sum_refs[:levels])
+    token_sums = [
+        Reduction(token_stages, sum_refs[i * levels : (i + 1) * levels]) for i in range(2)
+    ]
+    sum_refs = sum_refs[2 * levels :]
     early_sum, late_sum, last_sum = [
-        Reduction(grad_stages, sum_refs[levels + i * levels_g : levels + (i + 1) * levels_g])
-        for i in range(3)
+        Reduction(grad_stages, sum_refs[i * levels_g : (i + 1) * levels_g]) for i in range(3)
     ]
 
     pairs = (
@@ -350,7 +352,7 @@
     def cut(index):
         return pl.ds(pl.multiple_of(index * CHUNK, CHUNK), CHUNK)
 
-    def forward(index, carry):
+    def project(index, carry):
         part = cut(index)
         cells = cells_ref[part, :]
         projected = mm(cells, wx_ref[...]).astype(BF16)
@@ -359,61 +361,58 @@
         temp_lin = mm(projected, temp_bd[...])
         away = jnp.exp(-jnp.abs(temp_lin))
         temper = 0.5 + (jnp.maximum(temp_lin, 0.0) + jnp.log(1.0 + away))
-        inverse = 1.0 / temper
-        sigmoid = jnp.where(temp_lin >= 0.0, 1.0, away) / (1.0 + away)
         proj_ref[part, :] = projected
-        inverse_ref[part, :] = inverse
-        sigmoid_ref[part, :] = sigmoid
-        inverse_high, inverse_low = split(inverse)
+        inverse_ref[part, :] = 1.0 / temper
+        sigmoid_ref[part, :] = jnp.where(temp_lin >= 0.0, 1.0, away) / (1.0 + away)
+        for half in range(2):
+            lanes = slice(half * HALF, (half + 1) * HALF)
+            pair_ref[part, half * 256 : half * 256 + HALF] = d_hidden[:, lanes]
+            pair_ref[part, half * 256 + HALF : half * 256 + 256] = features[:, lanes]
+        return carry
+
+    def forward(half, index, carry):
+        part = cut(index)
+        lanes = slice(half * HALF, (half + 1) * HALF)
+        span = slice(half * 256, (half + 1) * 256)
         place = lax.broadcasted_iota(jnp.int32, (CHUNK, 1), 0) + index * CHUNK
         live = (place < count).astype(F32)
-        for half in range(2):
-            lanes = slice(half * HALF, (half + 1) * HALF)
-            span = slice(half * 256, (half + 1) * 256)
-            bent = jnp.tanh(mm(projected[:, lanes], slice_bd[...]) * 0.1)
-            cool = mm(inverse_high, spread_heads[half]) + mm(inverse_low, spread_heads[half])
-            scaled = (10.0 * bent) * cool
-            powers = jnp.exp(scaled)
-            sums = pick2(powers, same_head[...])
-            over = pl.reciprocal(sums, approx=True)
-            over = over * (2.0 - sums * over)
-            probs = powers * (live * over)
-            weights = probs.astype(BF16)
-            weight_ref[part, span] = weights
-            prob_ref[part, span] = probs
-            slope_ref[part, span] = (1.0 - bent * bent) * cool
-            scaled_ref[part, span] = scaled
-            pair = jnp.concatenate([d_hidden[:, lanes], features[:, lanes]], axis=1)
-            pair_ref[part, span] = pair
-            right = jnp.concatenate([pair, jnp.ones((CHUNK, 128), BF16)], axis=1)
-            acc_tokens[half] += mm_tn(weights, right)
+        bent = jnp.tanh(mm(proj_ref[part, lanes], slice_bd[...]) * 0.1)
+        cool = pick2(inverse_ref[part, :], spread_heads[half])
+        scaled = (10.0 * bent) * cool
+        powers = jnp.exp(scaled)
+        sums = pick2(powers, same_head[...])
+        over = pl.reciprocal(sums, approx=True)
+        over = over * (2.0 - sums * over)
+        probs = powers * (live * over)
+        weights = probs.astype(BF16)
+        weight_ref[part, span] = weights
+        prob_ref[part, span] = probs
+        slope_ref[part, span] = (1.0 - bent * bent) * cool
+        scaled_ref[part, span] = scaled
+        right = jnp.concatenate([pair_ref[part, span], jnp.ones((CHUNK, 128), BF16)], axis=1)
+        acc_tokens[half] += mm_tn(weights, right)
         return carry
 
-    lax.fori_loop(0, chunks, forward, 0)
-
-    payload = token_sum.source()
     lane = lax.broadcasted_iota(jnp.int32, (SLICES, 128), 1)
-    totals = jnp.zeros((SLICES, 128), F32)
-    for half in range(2):
-        lanes = slice(half * HALF, (half + 1) * HALF)
+
+    def pay(half):
+        payload = token_sums[half].source()
         dmix = jnp.where(half_diag, acc_tokens[half, :, 0:HALF], 0.0)
         numer = jnp.where(half_diag, acc_tokens[half, :, HALF : 2 * HALF], 0.0)
-        payload[0:SLICES, lanes] = sum(numer[i * 64 : i * 64 + 64] for i in range(4))
-        payload[SLICES : 2 * SLICES, lanes] = sum(dmix[i * 64 : i * 64 + 64] for i in range(4))
+        payload[0:SLICES, 0:HALF] = sum(numer[i * 64 : i * 64 + 64] for i in range(4))
+        payload[SLICES : 2 * SLICES, 0:HALF] = sum(dmix[i * 64 : i * 64 + 64] for i in range(4))
+        totals = jnp.zeros((SLICES, 128), F32)
         for i in range(4):
             block = acc_tokens[half, i * 64 : i * 64 + 64, 2 * HALF : 2 * HALF + 128]
-            totals = totals + jnp.where(lane == half * 4 + i, block, 0.0)
-    payload[0:SLICES, WIDTH : WIDTH + 128] = totals
-    payload[SLICES : 2 * SLICES, WIDTH : WIDTH + 128] = jnp.zeros((SLICES, 128), F32)
-
-    pl.semaphore_wait(barrier, greeted)
-    diag_square = block_mask((WIDTH, WIDTH), HEAD, HEAD)
+            totals = totals + jnp.where(lane == i, block, 0.0)
+        payload[0:SLICES, HALF : HALF + 128] = totals
+        payload[SLICES : 2 * SLICES, HALF : HALF + 128] = jnp.zeros((SLICES, 128), F32)
+
+    diag_square = block_mask((HALF, HALF), HEAD, HEAD)
 
     def prepare_maps():
         for k in range(3):
             square = mm(mm_tn(repeat32, wqkv_ref[k]).astype(BF16), repeat32)
-            square = jnp.concatenate([square, square], axis=0)
-            square = jnp.concatenate([square, square], axis=1)
             maps_ref[k] = jnp.where(diag_square, square, 0.0).astype(BF16)
         slice_t[...] = slice_bd[...].T
         wx_t[...] = wx_ref[...].T
@@ -424,32 +423,20 @@
             part = slice(index * CHUNK, (index + 1) * CHUNK)
             target[:, part] = source[part, :].T
 
-    fillers = [
-        prepare_maps,
-        functools.partial(turn, cells_ref, cells_t),
-        functools.partial(turn, cot_ref, cot_t),
-        functools.partial(turn, proj_ref, proj_t),
-    ]
-    for index in range(len(token_stages)):
-        token_sum.send(index)
-        if fillers:
-            fillers.pop(0)()
-        token_sum.fold(index)
-    for index in reversed(range(len(token_stages))):
-        token_sum.gather(index)
-        if fillers:
-            fillers.pop(0)()
-        token_sum.settle(index)
-    for filler in fillers:
-        filler()
-
-    total = token_sum.total()
-    numerators = total[0:SLICES, 0:WIDTH]
-    d_mixed = total[SLICES : 2 * SLICES, 0:WIDTH]
-    spread32 = block_mask((128, WIDTH), 1, HEAD).astype(BF16)
-    denominators = pick3(total[0:SLICES, WIDTH : WIDTH + 128], spread32) + 1e-05
-    tokens = numerators / denominators
-    queries, key_rows, value_rows = [pick2(tokens, maps_ref[k]) for k in range(3)]
+    def steps(reduction):
+        count_of_stages = len(reduction.stages)
+        for index in range(count_of_stages):
+            reduction.send(index)
+            yield
+            reduction.fold(index)
+        for index in reversed(range(count_of_stages)):
+            reduction.gather(index)
+            yield
+            reduction.settle(index)
+
+    def finish(moves):
+        for _ in moves:
+            pass
 
     def expand(value):
         return jnp.where(half_diag, jnp.concatenate([value] * 4, axis=0), 0.0)
@@ -458,67 +445,63 @@
         value = jnp.where(half_diag, value, 0.0)
         return sum(value[i * SLICES : (i + 1) * SLICES] for i in range(4))
 
-    root = 1.0 / math.sqrt(HEAD)
-    halves = [slice(half * HALF, (half + 1) * HALF) for half in range(2)]
-    keys_bd = [expand(key_rows[:, lanes]) for lanes in halves]
-    values_bd = [expand(value_rows[:, lanes]) for lanes in halves]
-    d_attention = [wide(d_mixed[:, halves[i]], values_bd[i], mm_nt) for i in range(2)]
-    bent = [
-        jnp.tanh(wide(queries[:, halves[i]], keys_bd[i], mm_nt) * root / 10.0) for i in range(2)
-    ]
-    powers = [jnp.exp(10.0 * value) for value in bent]
-    attention = [value / pick2(value, same_head[...]) for value in powers]
-    for i in range(2):
-        mixed = wide(attention[i], values_bd[i], mm)
-        both_bd[i, :, 0:HALF] = expand(mixed).astype(BF16)
-    shared = [attention[i] * d_attention[i] for i in range(2)]
-    shared = [shared[i] - attention[i] * pick2(shared[i], same_head[...]) for i in range(2)]
-    d_scores = [shared[i] * (1.0 - bent[i] * bent[i]) * root for i in range(2)]
-    d_queries = jnp.concatenate([wide(d_scores[i], keys_bd[i], mm) for i in range(2)], axis=1)
-    d_keys = jnp.concatenate(
-        [contract(wide(d_scores[i], queries[:, halves[i]], mm_tn)) for i in range(2)], axis=1
-    )
-    d_values = jnp.concatenate(
-        [contract(wide(attention[i], d_mixed[:, halves[i]], mm_tn)) for i in range(2)], axis=1
-    )
-    d_maps = (d_queries, d_keys, d_values)
-
     def pick_back(value, weight):
         high, low = split(value)
         return mm_nt(high, weight) + mm_nt(low, weight)
 
-    d_tokens = sum(pick_back(d_maps[k], maps_ref[k]) for k in range(3))
-    d_numer = d_tokens / denominators
-    away = d_numer * tokens
-    d_denom = []
-    for i in range(2):
-        both_bd[i, :, HALF : 2 * HALF] = expand(d_numer[:, halves[i]]).astype(BF16)
-        high, low = split(expand(away[:, halves[i]]))
+    root = 1.0 / math.sqrt(HEAD)
+
+    def attend(half):
+        total = token_sums[half].total()
+        numerators = total[0:SLICES, 0:HALF]
+        d_mixed = total[SLICES : 2 * SLICES, 0:HALF]
+        spread32 = block_mask((128, HALF), 1, HEAD).astype(BF16)
+        denominators = pick3(total[0:SLICES, HALF : HALF + 128], spread32) + 1e-05
+        tokens = numerators / denominators
+        queries, key_rows, value_rows = [pick2(tokens, maps_ref[k]) for k in range(3)]
+        keys_bd = expand(key_rows)
+        values_bd = expand(value_rows)
+        d_attention = wide(d_mixed, values_bd, mm_nt)
+        bent = jnp.tanh(wide(queries, keys_bd, mm_nt) * (root / 10.0))
+        powers = jnp.exp(10.0 * bent)
+        attention = powers / pick2(powers, same_head[...])
+        mixed_half = expand(wide(attention, values_bd, mm)).astype(BF16)
+        shared = attention * d_attention
+        shared = shared - attention * pick2(shared, same_head[...])
+        d_scores = shared * (1.0 - bent * bent) * root
+        d_queries = wide(d_scores, keys_bd, mm)
+        d_keys = contract(wide(d_scores, queries, mm_tn))
+        d_values = contract(wide(attention, d_mixed, mm_tn))
+        d_maps = (d_queries, d_keys, d_values)
+        d_tokens = sum(pick_back(d_maps[k], maps_ref[k]) for k in range(3))
+        d_numer = d_tokens / denominators
+        dnumer_half = expand(d_numer).astype(BF16)
+        both = jnp.concatenate([mixed_half, dnumer_half], axis=1)
+        both_bd[half] = both
+        both_t[half] = both.T
+        high, low = split(expand(d_numer * tokens))
         ones = jnp.ones((128, HALF), BF16)
-        d_denom.append(-(mm_nt(ones, high) + mm_nt(ones, low))[0:1, :])
-
-    for half in range(2):
-        both_t[half] = both_bd[half].T
-
-    def early(index, carry):
+        d_denom = -(mm_nt(ones, high) + mm_nt(ones, low))[0:1, :]
+        return tokens, d_maps, d_denom
+
+    def early(half, index, carry):
         part = cut(index)
-        for half in range(2):
-            lanes = slice(half * HALF, (half + 1) * HALF)
-            made = mm(weight_ref[part, half * 256 : (half + 1) * 256], both_bd[half]).astype(BF16)
-            hidden_ref[part, lanes] = made[:, 0:HALF]
-            dfeat_ref[part, lanes] = made[:, HALF : 2 * HALF]
+        lanes = slice(half * HALF, (half + 1) * HALF)
+        made = mm(weight_ref[part, half * 256 : (half + 1) * 256], both_bd[half]).astype(BF16)
+        hidden_ref[part, lanes] = made[:, 0:HALF]
+        dfeat_ref[part, lanes] = made[:, HALF : 2 * HALF]
         return carry
 
-    lax.fori_loop(0, chunks, early, 0)
-    source = early_sum.source()
-    source[:, 0:WIDTH] = mm(cot_t[...], hidden_ref[...]).astype(BF16)
-    source[:, WIDTH : 2 * WIDTH] = mm(cells_t[...], dfeat_ref[...]).astype(BF16)
-
-    def backward(half, index, carry):
+    def fill_early(half, target):
+        lanes = slice(half * HALF, (half + 1) * HALF)
+        target[:, 0:128] = mm(cot_t[...], hidden_ref[:, lanes]).astype(BF16)
+        target[:, 128:256] = mm(cells_t[...], dfeat_ref[:, lanes]).astype(BF16)
+
+    def backward(half, d_denom, index, carry):
         part = cut(index)
         lanes = slice(half * HALF, (half + 1) * HALF)
         span = slice(half * 256, (half + 1) * 256)
-        d_weights = mm(pair_ref[part, span], both_t[half]) + d_denom[half]
+        d_weights = mm(pair_ref[part, span], both_t[half]) + d_denom
         probs = prob_ref[part, span]
         shared = probs * d_weights
         shared = shared - probs * pick2(shared, same_head[...])
@@ -532,7 +515,7 @@
         ).astype(BF16)
         return carry
 
-    def fill(half, target):
+    def fill_late(half, target, start):
         lanes = slice(half * HALF, (half + 1) * HALF)
         block = mm(proj_t[lanes, :], dlogit_ref[...])
         block = jnp.where(block_mask((HALF, 256), HEAD, SLICES), block, 0.0)
@@ -542,9 +525,10 @@
         heads = lax.broadcasted_iota(jnp.int32, (HALF, 128), 0) // HEAD + 4 * half
         own = jnp.where(here == heads, mm(proj_t[lanes, :], dtemp_ref[...]), 0.0)
         own = jnp.sum(own, axis=1, keepdims=True)
-        target[:, 0:128] = mm(cells_t[...], dproj_ref[:, lanes]).astype(BF16)
-        target[0:HALF, 128:256] = jnp.where(here < SLICES, block, own).astype(BF16)
-        target[HALF:WIDTH, 128:256] = jnp.zeros((WIDTH - HALF, 128), BF16)
+        extra = slice(start + 128, start + 256)
+        target[:, start : start + 128] = mm(cells_t[...], dproj_ref[:, lanes]).astype(BF16)
+        target[0:HALF, extra] = jnp.where(here < SLICES, block, own).astype(BF16)
+        target[HALF:WIDTH, extra] = jnp.zeros((WIDTH - HALF, 128), BF16)
 
     def results(index, carry):
         part = cut(index)
@@ -558,60 +542,85 @@
         ).astype(BF16)
         return carry
 
-    def steps(reduction):
-        for index in range(len(grad_stages)):
-            reduction.send(index)
-            yield
-            reduction.fold(index)
-        for index in reversed(range(len(grad_stages))):
-            reduction.gather(index)
-            yield
-            reduction.settle(index)
-
-    early_steps, late_steps, last_steps = steps(early_sum), steps(late_sum), steps(last_sum)
-    next(early_steps)
-    lax.fori_loop(0, middle, functools.partial(backward, 0), 0)
-    next(early_steps)
-    lax.fori_loop(middle, chunks, functools.partial(backward, 0), 0)
-    fill(0, late_sum.source())
-    next(late_steps)
-    next(early_steps)
-    lax.fori_loop(0, middle, functools.partial(backward, 1), 0)
-    next(late_steps)
-    next(early_steps)
-    lax.fori_loop(middle, chunks, functools.partial(backward, 1), 0)
-    fill(1, last_sum.source())
-    next(last_steps)
-    next(late_steps)
-    lax.fori_loop(0, chunks, cell_grads, 0)
+    def loop(step, first=0, end=chunks):
+        lax.fori_loop(first, end, step, 0)
+
+    bind = functools.partial
+    loop(project)
+    loop(bind(forward, 0))
+    pay(0)
+    pl.semaphore_wait(barrier, greeted)
+    first_moves, second_moves = [steps(reduction) for reduction in token_sums]
+    next(first_moves)
+    loop(bind(forward, 1), 0, middle)
+    next(first_moves)
+    loop(bind(forward, 1), middle, chunks)
+    pay(1)
+    next(second_moves)
+    next(first_moves)
+    prepare_maps()
+    turn(cells_ref, cells_t)
+    next(second_moves)
+    next(first_moves)
+    turn(cot_ref, cot_t)
+    turn(proj_ref, proj_t)
+    finish(first_moves)
+
+    tokens0, d_maps0, d_denom0 = attend(0)
+    next(second_moves)
+    loop(bind(early, 0))
+    loop(bind(backward, 0, d_denom0), 0, middle)
+    next(second_moves)
+    loop(bind(backward, 0, d_denom0), middle, chunks)
+    fill_early(0, early_sum.source())
+    fill_late(0, early_sum.source(), 256)
+    early_moves, late_moves, last_moves = [
+        steps(reduction) for reduction in (early_sum, late_sum, last_sum)
+    ]
+    next(early_moves)
+    finish(second_moves)
+
+    tokens1, d_maps1, d_denom1 = attend(1)
+    next(early_moves)
+    loop(bind(early, 1))
+    fill_early(1, late_sum.source())
+    next(late_moves)
+    loop(bind(backward, 1, d_denom1), 0, middle)
+    next(early_moves)
+    next(late_moves)
+    loop(bind(backward, 1, d_denom1), middle, chunks)
+    fill_late(1, last_sum.source(), 0)
+    next(last_moves)
+    next(early_moves)
+    next(late_moves)
+    loop(cell_grads)
     put(gcells_ref, gcells_hbm)
-    next(last_steps)
-    for _ in early_steps:
-        pass
-    lax.fori_loop(0, chunks, results, 0)
+    next(last_moves)
+    finish(early_moves)
+    next(late_moves)
+    loop(results)
     put(result_ref, result_hbm)
-    gwfx_ref[...] = early_sum.total()[:, WIDTH : 2 * WIDTH].astype(F32) * scale
-    put(gwfx_ref, gwfx_hbm)
-    gout_ref[...] = early_sum.total()[:, 0:WIDTH].astype(F32).T * scale
-    put(gout_ref, gout_hbm)
-    next(late_steps)
     for k in range(3):
-        square = jnp.where(diag_square, wide(tokens, d_maps[k], mm_tn), 0.0)
-        strip = sum(square[i * HEAD : (i + 1) * HEAD] for i in range(HEADS))
-        strip = strip[:, 0:HALF] + strip[:, HALF:WIDTH]
+        square = wide(tokens0, d_maps0[k], mm_tn) + wide(tokens1, d_maps1[k], mm_tn)
+        square = jnp.where(diag_square, square, 0.0)
+        strip = sum(square[i * HEAD : (i + 1) * HEAD] for i in range(4))
         gqkv_ref[k] = pick2(strip, repeat32.T) * scale
     put(gqkv_ref, gqkv_hbm)
-    next(last_steps)
-    for _ in late_steps:
-        pass
-    gwx_ref[:, 0:HALF] = late_sum.total()[:, 0:HALF].astype(F32) * scale
-    for _ in last_steps:
-        pass
+    gwfx_ref[:, 0:HALF] = early_sum.total()[:, 128:256].astype(F32) * scale
+    gout_ref[0:HALF, :] = early_sum.total()[:, 0:128].astype(F32).T * scale
+    gwx_ref[:, 0:HALF] = early_sum.total()[:, 256:384].astype(F32) * scale
+    next(last_moves)
+    finish(late_moves)
+    gwfx_ref[:, HALF:WIDTH] = late_sum.total()[:, 128:256].astype(F32) * scale
+    put(gwfx_ref, gwfx_hbm)
+    gout_ref[HALF:WIDTH, :] = late_sum.total()[:, 0:128].astype(F32).T * scale
+    put(gout_ref, gout_hbm)
+    next(last_moves)
+    finish(last_moves)
     gwx_ref[:, HALF:WIDTH] = last_sum.total()[:, 0:HALF].astype(F32) * scale
     put(gwx_ref, gwx_hbm)
-    extra = sum(
-        reduction.total()[0:HALF, 128:256].astype(F32) for reduction in (late_sum, last_sum)
-    )
+    extra = early_sum.total()[0:HALF, 384:512].astype(F32)
+    extra = extra + last_sum.total()[0:HALF, 128:256].astype(F32)
     extra = sum(extra[i * HEAD : (i + 1) * HEAD] for i in range(4)) * scale
     gslice_ref[...] = extra[:, 0:SLICES]
     put(gslice_ref, gslice_hbm)
@@ -699,7 +708,7 @@
             vmem((WIDTH, 128), BF16),
             vmem((128, WIDTH), BF16),
             vmem((256, 256), BF16),
-            vmem((3, WIDTH, WIDTH), BF16),
+            vmem((3, HALF, HALF), BF16),
             vmem((2, 256, 2 * HALF + 128), F32),
             vmem((2, 256, 2 * HALF), BF16),
             vmem((2, 256, 2 * HALF), BF16),
@@ -708,7 +717,7 @@
             vmem((WIDTH, WIDTH), BF16),
             vmem((WIDTH, WIDTH), BF16),
         ]
-        + Reduction.scratch(token_stages, WIDTH + 128, F32)
+        + Reduction.scratch(token_stages, HALF + 128, F32) * 2
         + Reduction.scratch(grad_stages, 2 * WIDTH, BF16)
         + Reduction.scratch(grad_stages, 256, BF16)
         + Reduction.scratch(grad_stages, 256, BF16),

time: 57.1 us -> 59.1 us (1.035)
  Pallas kernels: 55.6 us -> 57.6 us
    pallas_call x1, Pallas kernels: 53.1 us -> 55.2 us  [body(): pl.pallas_call(functools.partial(layer_kernel, token_stages, grad_stages,...]
where the time goes in v4:
time: 59.1 us; the launch traced here: 58.9 us
  Pallas kernels  57.6 us (97%)
  between operations  1.29 us (2%)
    pallas_call x1, Pallas kernels, body(): pl.pallas_call(functools.partial(layer_kernel, token_stages, grad_stages,...  55.2 us
    pallas_call x1, Pallas kernels, body(): pl.pallas_call(hand_over, out_shape=out_shape, in_specs=[anywhere] * 8, o...  2.43 us

profile of v4, /device:TPU:0, one launch (start us, length us, event | category | flops | bytes accessed | tf_op | source)
XLA Modules:
  0.0 58.9 jit_solution(9496100101504790705)
XLA Ops:
  1.3 55.2 %shard_map.152 = (bf16[1024,256]{1,0:T(8,128)(2,1)}, bf16[1024,256]{1,0:T(8,128)(2,1)}, f32[256,256]{1,0:T(8,128)}, f32[256,256]{1,0:T(8,128)}, f32[32,64]{1,0:T...) custom-call(s32[1]{0:T(128)S(6)} %copy.17.counts_hbm, bf16[1024,256]{1,0:T(8,128)(2,1)} %cells_hbm.1, ...), custom_call_target="tpu_custom_call" | custom-call | tf_op jit(solution)/shard_map/pallas_call | solution.py:671
  56.5 2.4 %shard_map.153 = (bf16[1024,256]{1,0:T(8,128)(2,1)}, bf16[1024,256]{1,0:T(8,128)(2,1)}, f32[256,256]{1,0:T(8,128)}, f32[256,256]{1,0:T(8,128)}, f32[32,64]{1,0:T...) custom-call(bf16[1024,256]{1,0:T(8,128)(2,1)} %get-tuple-element.24.refs_0_, ...), custom_call_target="tpu_custom_call" | custom-call | tf_op jit(solution)/shard_map/pallas_call | solution.py:728

commit v5 on v4

--- a/solution.py
+++ b/solution.py
@@ -343,18 +343,19 @@
         heads = lax.broadcasted_iota(jnp.int32, (128, HALF), 1) // HEAD + 4 * half
         here = lax.broadcasted_iota(jnp.int32, (128, HALF), 0)
         temp_row[:, place] = jnp.where(here == heads, line, 0.0).astype(BF16)
-    acc_tokens[...] = jnp.zeros_like(acc_tokens)
     for copy in incoming[2:]:
         copy.wait()
     wout_t[...] = wout_ref[...].T
     count = counts_ref[0]
 
     def cut(index):
-        return pl.ds(pl.multiple_of(index * CHUNK, CHUNK), CHUNK)
+        return slice(index * CHUNK, (index + 1) * CHUNK)
 
     def project(index, carry):
         part = cut(index)
         cells = cells_ref[part, :]
+        cells_t[:, part] = cells.T
+        cot_t[:, part] = cot_ref[part, :].T
         projected = mm(cells, wx_ref[...]).astype(BF16)
         features = mm(cells, wfx_ref[...]).astype(BF16)
         d_hidden = mm(cot_ref[part, :], wout_t[...]).astype(BF16)
@@ -362,6 +363,7 @@
         away = jnp.exp(-jnp.abs(temp_lin))
         temper = 0.5 + (jnp.maximum(temp_lin, 0.0) + jnp.log(1.0 + away))
         proj_ref[part, :] = projected
+        proj_t[:, part] = projected.T
         inverse_ref[part, :] = 1.0 / temper
         sigmoid_ref[part, :] = jnp.where(temp_lin >= 0.0, 1.0, away) / (1.0 + away)
         for half in range(2):
@@ -389,14 +391,15 @@
         prob_ref[part, span] = probs
         slope_ref[part, span] = (1.0 - bent * bent) * cool
         scaled_ref[part, span] = scaled
-        right = jnp.concatenate([pair_ref[part, span], jnp.ones((CHUNK, 128), BF16)], axis=1)
-        acc_tokens[half] += mm_tn(weights, right)
         return carry
 
     lane = lax.broadcasted_iota(jnp.int32, (SLICES, 128), 1)
 
     def pay(half):
         payload = token_sums[half].source()
+        span = slice(half * 256, (half + 1) * 256)
+        right = jnp.concatenate([pair_ref[:, span], jnp.ones((rows, 128), BF16)], axis=1)
+        acc_tokens[half] = mm_tn(weight_ref[:, span], right)
         dmix = jnp.where(half_diag, acc_tokens[half, :, 0:HALF], 0.0)
         numer = jnp.where(half_diag, acc_tokens[half, :, HALF : 2 * HALF], 0.0)
         payload[0:SLICES, 0:HALF] = sum(numer[i * 64 : i * 64 + 64] for i in range(4))
@@ -417,11 +420,6 @@
         slice_t[...] = slice_bd[...].T
         wx_t[...] = wx_ref[...].T
         wfx_t[...] = wfx_ref[...].T
-
-    def turn(source, target):
-        for index in range(chunks):
-            part = slice(index * CHUNK, (index + 1) * CHUNK)
-            target[:, part] = source[part, :].T
 
     def steps(reduction):
         count_of_stages = len(reduction.stages)
@@ -543,7 +541,8 @@
         return carry
 
     def loop(step, first=0, end=chunks):
-        lax.fori_loop(first, end, step, 0)
+        for index in range(first, end):
+            step(index, 0)
 
     bind = functools.partial
     loop(project)
@@ -559,11 +558,8 @@
     next(second_moves)
     next(first_moves)
     prepare_maps()
-    turn(cells_ref, cells_t)
     next(second_moves)
     next(first_moves)
-    turn(cot_ref, cot_t)
-    turn(proj_ref, proj_t)
     finish(first_moves)
 
     tokens0, d_maps0, d_denom0 = attend(0)

time: 59.1 us -> 55.3 us (0.936)
  Pallas kernels: 57.6 us -> 53.8 us
    pallas_call x1, Pallas kernels: 55.2 us -> 51.3 us  [body(): pl.pallas_call(functools.partial(layer_kernel, token_stages, grad_stages,...]
where the time goes in v5:
time: 55.3 us; the launch traced here: 55.1 us
  Pallas kernels  53.8 us (97%)
  between operations  1.29 us (2%)
    pallas_call x1, Pallas kernels, body(): pl.pallas_call(functools.partial(layer_kernel, token_stages, grad_stages,...  51.3 us
    pallas_call x1, Pallas kernels, body(): pl.pallas_call(hand_over, out_shape=out_shape, in_specs=[anywhere] * 8, o...  2.43 us

profile of v5, /device:TPU:0, one launch (start us, length us, event | category | flops | bytes accessed | tf_op | source)
XLA Modules:
  0.0 55.1 jit_solution(9976494804907340808)
XLA Ops:
  1.3 51.3 %shard_map.152 = (bf16[1024,256]{1,0:T(8,128)(2,1)}, bf16[1024,256]{1,0:T(8,128)(2,1)}, f32[256,256]{1,0:T(8,128)}, f32[256,256]{1,0:T(8,128)}, f32[32,64]{1,0:T...) custom-call(s32[1]{0:T(128)S(6)} %copy.17.counts_hbm, bf16[1024,256]{1,0:T(8,128)(2,1)} %cells_hbm.1, ...), custom_call_target="tpu_custom_call" | custom-call | tf_op jit(solution)/shard_map/pallas_call | solution.py:667
  52.6 2.4 %shard_map.153 = (bf16[1024,256]{1,0:T(8,128)(2,1)}, bf16[1024,256]{1,0:T(8,128)(2,1)}, f32[256,256]{1,0:T(8,128)}, f32[256,256]{1,0:T(8,128)}, f32[32,64]{1,0:T...) custom-call(bf16[1024,256]{1,0:T(8,128)(2,1)} %get-tuple-element.24.refs_0_, ...), custom_call_target="tpu_custom_call" | custom-call | tf_op jit(solution)/shard_map/pallas_call | solution.py:724
